TPU v7x, 32 devices: a whole 2x2x4 slice. The times are simulated.
32 devices in a mesh: rows: 4 (over y, x), mp: 8 (over z, core).
Axes of the slice: x: 2, y: 2, z: 4, core: 2. Of those that a mesh axis runs over, the one named last changes fastest.
Arguments:
- tokens: bfloat16 [32768, 1024], P(('rows', 'mp')), may hold values from -6 to 6
- qkv_weight: bfloat16 [3, 1024, 1024], P(None, None, 'mp'), may hold values from -0.1875 to 0.1875
- qv_bias: bfloat16 [2, 1024], P(None, 'mp'), may hold values from -1.1953125 to 1.1953125
- out_weight: bfloat16 [1024, 1024], P('mp'), may hold values from -0.75 to 0.75
- up_weight: bfloat16 [1024, 4096], P(None, 'mp'), may hold values from -0.1875 to 0.1875
- up_bias: bfloat16 [4096], P('mp'), may hold values from -1.1953125 to 1.1953125
- down_weight: bfloat16 [4096, 1024], P('mp'), may hold values from -0.09375 to 0.09375
- norm_gains: bfloat16 [2, 1024], replicated, may hold values from 0.5 to 1.5
- shift_vectors: bfloat16 [4, 1024], replicated, may hold values from -1.1953125 to 1.1953125
- lengths: int32 [32, 6], P('rows'), may hold values from 1 to 1019, as said below
- cotangent: bfloat16 [32768, 1024], P(('rows', 'mp')), may hold values from -6 to 6
Outputs:
- mixed: bfloat16 [32768, 1024], P(('rows', 'mp'))
- block_loss: float32 [32], P('rows')
- input_grad: float32 [32768, 1024], P(('rows', 'mp'))
- qkv_grad: float32 [3, 1024, 1024], P(None, None, 'mp')
- qv_bias_grad: float32 [2, 1024], P(None, 'mp')
- out_weight_grad: float32 [1024, 1024], P('mp')
- up_weight_grad: float32 [1024, 4096], P(None, 'mp')
- up_bias_grad: float32 [4096], P('mp')
- down_weight_grad: float32 [4096, 1024], P('mp')
- vector_grad: float32 [6, 1024], P(None, 'mp')
Inputs may be any that keep to these rules, and one draw needn't show every extreme that they name: Each block's 6 documents fill its first slots in order and the rest of the block is padding; a block's lengths sum to at most 1024. In at least one block the lengths sum to exactly 1024, and one of its documents has 1019 slots.
All inputs are finite; a program needn't handle non-finite values.
Results may differ from a plain program's by a relative error of at most 0.012.
The roundings to bfloat16 on the way count: a program that leaves them out, or rounds other values in their place, can miss the bound.
Values may be sent and summed in bfloat16 or wider, within the bound.
No kernel may reach another device: no remote copies, remote signals or barrier semaphores. Data moves between devices by JAX's collectives and lax.ppermute only.
A program may use at most 512 MiB of HBM per device.

v0:
```python
import math

import jax
import jax.numpy as jnp
from jax import lax
from jax.sharding import PartitionSpec as P

HD = 64
SLOTS = 1024
DOCS = 6


EPSILON = 1e-05
MASKED = -1e30


def layer_norm(values, gain, shift):
    center = jnp.mean(values, axis=-1, keepdims=True)
    spread = values - center
    variance = jnp.mean(spread * spread, axis=-1, keepdims=True)
    return spread * lax.rsqrt(variance + EPSILON) * gain + shift


def norm_back(values, gain, shift, grad):
    return jax.vjp(layer_norm, values, gain, shift)[1](grad)


def gelu_tanh(values):
    return jax.nn.gelu(values, approximate=True)


def gelu_back(values, grad):
    return jax.vjp(gelu_tanh, values)[1](grad)[0]


def document_ids(lengths):
    endings = jnp.cumsum(lengths, axis=1)
    position = jnp.arange(SLOTS, dtype=jnp.int32)
    segment = jnp.sum((position[None, :, None] >= endings[:, None, :]).astype(jnp.int32), axis=2)
    living = segment < DOCS
    identity = jnp.where(living, segment, DOCS + position[None, :])
    return (identity, living)


def times_back(left, right):
    return lax.dot_general(
        left, right, (((1,), (1,)), ((), ())), preferred_element_type=jnp.float32
    )


def over_rows(left, right):
    return lax.dot_general(
        left, right, (((0,), (0,)), ((), ())), preferred_element_type=jnp.float32
    )


def row_slice(array, start, count):
    return lax.dynamic_slice_in_dim(array, start, count, 0)


def allowed_pairs(identity, first, finish):
    position = jnp.arange(SLOTS)
    query_pos = position[first:finish]
    same = identity[first:finish, None] == identity[None, :finish]
    return same & (position[None, :finish] <= query_pos[:, None])


def block_scores(queries, key_rows, identity, first, finish):
    scores = jnp.einsum(
        "qhd,khd->hqk", queries[first:finish], key_rows[:finish], preferred_element_type=jnp.float32
    )
    return jnp.where(allowed_pairs(identity, first, finish)[None], scores, MASKED)


def attend_block(member):
    queries, key_rows, value_rows, identity = member
    block_span = min(512, SLOTS)
    outputs = []
    totals = []
    for first in range(0, SLOTS, block_span):
        finish = first + block_span
        scores = block_scores(queries, key_rows, identity, first, finish)
        highest = jnp.max(scores, axis=-1, keepdims=True)
        log_total = highest + jnp.log(jnp.sum(jnp.exp(scores - highest), axis=-1, keepdims=True))
        weights = jnp.exp(scores - log_total).astype(jnp.bfloat16)
        outputs.append(
            jnp.einsum(
                "hqk,khd->qhd", weights, value_rows[:finish], preferred_element_type=jnp.float32
            )
        )
        totals.append(log_total)
    return (jnp.concatenate(outputs, 0).astype(jnp.bfloat16), jnp.concatenate(totals, 1))


def attend_back(member):
    queries, key_rows, value_rows, identity, out_grad, log_totals = member
    block_span = min(512, SLOTS)
    query_parts = []
    key_grad = jnp.zeros(key_rows.shape, jnp.float32)
    value_grad = jnp.zeros(value_rows.shape, jnp.float32)
    for first in range(0, SLOTS, block_span):
        finish = first + block_span
        scores = block_scores(queries, key_rows, identity, first, finish)
        weights = jnp.exp(scores - log_totals[:, first:finish])
        rounded = weights.astype(jnp.bfloat16)
        grad_rows = out_grad[first:finish]
        prob_grad = jnp.einsum(
            "qhd,khd->hqk", grad_rows, value_rows[:finish], preferred_element_type=jnp.float32
        )
        balance = jnp.sum(prob_grad * weights, axis=-1, keepdims=True)
        score_grad = (weights * (prob_grad - balance)).astype(jnp.bfloat16)
        query_parts.append(
            jnp.einsum(
                "hqk,khd->qhd", score_grad, key_rows[:finish], preferred_element_type=jnp.float32
            )
        )
        key_grad = key_grad.at[:finish].add(
            jnp.einsum(
                "hqk,qhd->khd",
                score_grad,
                queries[first:finish],
                preferred_element_type=jnp.float32,
            )
        )
        value_grad = value_grad.at[:finish].add(
            jnp.einsum("hqk,qhd->khd", rounded, grad_rows, preferred_element_type=jnp.float32)
        )
    return (jnp.concatenate(query_parts, 0), key_grad, value_grad)


def body(
    tokens,
    qkv_weight,
    qv_bias,
    out_weight,
    up_weight,
    up_bias,
    down_weight,
    norm_gains,
    shift_vectors,
    lengths,
    cotangent,
):
    share = tokens.shape[0]
    width = tokens.shape[1]
    blocks_here = lengths.shape[0]
    group = blocks_here * SLOTS
    factor = HD ** (-0.5)
    identity, living = document_ids(lengths)
    offset = lax.axis_index("mp") * share
    live_rows = row_slice(living.reshape(group).astype(jnp.float32), offset, share)
    gains = norm_gains.astype(jnp.float32)
    shifts = shift_vectors.astype(jnp.float32)
    inputs = tokens.astype(jnp.float32)
    normed = layer_norm(inputs, gains[0], shifts[0]).astype(jnp.bfloat16)
    qkv_mats, qv_shift, out_mats = (qkv_weight, qv_bias, out_weight)
    attn_rows = lax.all_gather(normed, "mp", axis=0, tiled=True)
    attn_width = qkv_mats.shape[2]
    attn_heads = attn_width // HD
    attn_blocks = identity.shape[0]
    span_rows = attn_rows.shape[0]
    queries = (
        (
            jnp.dot(attn_rows, qkv_mats[0], preferred_element_type=jnp.float32)
            + qv_shift[0].astype(jnp.float32)
        )
        * factor
    ).astype(jnp.bfloat16)
    key_rows = jnp.dot(attn_rows, qkv_mats[1], preferred_element_type=jnp.float32).astype(
        jnp.bfloat16
    )
    value_rows = (
        jnp.dot(attn_rows, qkv_mats[2], preferred_element_type=jnp.float32)
        + qv_shift[1].astype(jnp.float32)
    ).astype(jnp.bfloat16)
    shaped = (attn_blocks, SLOTS, attn_heads, HD)
    attended, log_totals = lax.map(
        attend_block,
        (queries.reshape(shaped), key_rows.reshape(shaped), value_rows.reshape(shaped), identity),
    )
    attended = attended.reshape(span_rows, attn_width)
    middle = inputs + (
        lax.psum_scatter(
            jnp.dot(
                row_slice(attended, jnp.int32(0), share * lax.axis_size("mp")),
                out_weight,
                preferred_element_type=jnp.float32,
            ),
            "mp",
            scatter_dimension=0,
            tiled=True,
        )
        + shifts[1]
    )
    normed_two = layer_norm(middle, gains[1], shifts[2]).astype(jnp.bfloat16)
    weighting = cotangent.astype(jnp.float32) * live_rows[:, None]
    feed_grad = weighting.astype(jnp.bfloat16)
    normed_two_all = lax.all_gather(normed_two, "mp", axis=0, tiled=True)
    hidden = jnp.dot(
        normed_two_all, up_weight, preferred_element_type=jnp.float32
    ) + up_bias.astype(jnp.float32)
    active = gelu_tanh(hidden).astype(jnp.bfloat16)
    output = middle + (
        lax.psum_scatter(
            jnp.dot(
                row_slice(active, jnp.int32(0), share * lax.axis_size("mp")),
                down_weight,
                preferred_element_type=jnp.float32,
            ).astype(jnp.bfloat16),
            "mp",
            scatter_dimension=0,
            tiled=True,
        ).astype(jnp.float32)
        + shifts[3]
    )
    grad_all = lax.all_gather(feed_grad, "mp", axis=0, tiled=True)
    down_grad = over_rows(active, grad_all)
    active_grad = times_back(grad_all, down_weight)
    hidden_grad = gelu_back(hidden, active_grad).astype(jnp.bfloat16)
    up_grad = over_rows(normed_two_all, hidden_grad)
    up_bias_grad = jnp.sum(hidden_grad.astype(jnp.float32), axis=0)
    normed_two_grad = lax.psum_scatter(
        times_back(row_slice(hidden_grad, jnp.int32(0), share * lax.axis_size("mp")), up_weight),
        "mp",
        scatter_dimension=0,
        tiled=True,
    )
    row_block = (offset + jnp.arange(share)) // SLOTS
    membership = (row_block[:, None] == jnp.arange(blocks_here)[None, :]).astype(jnp.float32)
    part_loss = jnp.sum(membership * jnp.sum(output * weighting, axis=1)[:, None], axis=0)
    block_loss = lax.psum(part_loss, "mp") / math.sqrt(SLOTS * width)
    feed_shift = jnp.sum(weighting, axis=0)
    middle_part, gain_two, shift_two = norm_back(middle, gains[1], shifts[2], normed_two_grad)
    middle_grad = weighting + middle_part
    branch_grad = middle_grad.astype(jnp.bfloat16)
    attn_shift = jnp.sum(branch_grad.astype(jnp.float32), axis=0)
    branch_use = lax.all_gather(branch_grad, "mp", axis=0, tiled=True)
    out_full = over_rows(attended, branch_use)
    attended_grad = times_back(branch_use, out_mats).astype(jnp.bfloat16)
    query_grad, key_grad, value_grad = lax.map(
        attend_back,
        (
            queries.reshape(shaped),
            key_rows.reshape(shaped),
            value_rows.reshape(shaped),
            identity,
            attended_grad.reshape(shaped),
            log_totals,
        ),
    )
    query_grad = (query_grad.reshape(span_rows, attn_width) * factor).astype(jnp.bfloat16)
    key_grad = key_grad.reshape(span_rows, attn_width).astype(jnp.bfloat16)
    value_grad = value_grad.reshape(span_rows, attn_width).astype(jnp.bfloat16)
    qkv_full = jnp.stack(
        [
            over_rows(attn_rows, query_grad),
            over_rows(attn_rows, key_grad),
            over_rows(attn_rows, value_grad),
        ]
    )
    qv_full = jnp.stack(
        [
            jnp.sum(query_grad.astype(jnp.float32), axis=0),
            jnp.sum(value_grad.astype(jnp.float32), axis=0),
        ]
    )
    start = jnp.int32(0)
    total = times_back(row_slice(query_grad, start, share * lax.axis_size("mp")), qkv_weight[0])
    total = total + times_back(
        row_slice(key_grad, start, share * lax.axis_size("mp")), qkv_weight[1]
    )
    normed_grad = lax.psum_scatter(
        total
        + times_back(row_slice(value_grad, start, share * lax.axis_size("mp")), qkv_weight[2]),
        "mp",
        scatter_dimension=0,
        tiled=True,
    )
    qkv_grad, qv_bias_grad, out_grad = (qkv_full, qv_full, out_full)
    input_part, gain_one, shift_one = norm_back(inputs, gains[0], shifts[0], normed_grad)
    input_grad = middle_grad + input_part
    vectors = jnp.stack([gain_one, gain_two, shift_one, attn_shift, shift_two, feed_shift])
    vector_part = lax.psum_scatter(vectors, "mp", scatter_dimension=1, tiled=True)
    summed = lax.psum(
        (qkv_grad, qv_bias_grad, out_grad, up_grad, up_bias_grad, down_grad, vector_part), "rows"
    )
    return (
        output.astype(jnp.bfloat16),
        block_loss,
        input_grad,
        summed[0],
        summed[1],
        summed[2],
        summed[3],
        summed[4],
        summed[5],
        summed[6],
    )


def solution(mesh):
    placed = (
        P(("rows", "mp"), None),
        P(None, None, "mp"),
        P(None, "mp"),
        P("mp", None),
        P(None, "mp"),
        P("mp"),
        P("mp", None),
        P(),
        P(),
        P("rows", None),
        P(("rows", "mp"), None),
    )
    return jax.shard_map(
        body,
        mesh=mesh,
        in_specs=placed,
        out_specs=(
            P(("rows", "mp"), None),
            P("rows"),
            P(("rows", "mp"), None),
            P(None, None, "mp"),
            P(None, "mp"),
            P("mp", None),
            P(None, "mp"),
            P("mp"),
            P("mp", None),
            P(None, "mp"),
        ),
        check_vma=False,
    )
```

profile of v0, /device:TPU:0, one launch (start us, length us, event | category | flops | bytes accessed | tf_op | source)
XLA Modules:
  0.0 2464.1 jit_solution(5087401129593394133)
XLA Ops:
  15.6 153.5 %all-gather.5.cloned.1.call-done = bf16[8192,1024]{1,0:T(8,128)(2,1)} async-done(((bf16[1024,1024]{1,0:T(8,128)(2,1)}), bf16[8192,1024]{1,0:T(8,128)(2,1)}) %all-gather.5.cloned.1.call-update) | async-done | bytes 16777232 | tf_op jit(solution)/shard_map/all_gather | solution.py:157
  169.1 11.6 fusion.75
  180.7 8.7 reshape.648
  189.4 10.6 copy.59
  200.0 11.6 fusion.74
  211.6 8.2 reshape.649
  219.8 10.8 copy.60
  230.6 11.6 convolution_convert_fusion.3
  242.2 8.2 reshape.650
  250.4 10.6 copy.61
  261.1 89.5 %while.35 = (s32[]{:T(128)}, bf16[8,1024,2,64]{1,3,2,0:T(8,128)(2,1)}, f32[8,2,1024,1]{2,1,3,0:T(2,128)}, bf16[8,1024,2,64]{1,3,2,0:T(8,128)(2,1)}, s32[8,1024]{...) while((s32[]{:T(128)}, ...), condition=%wide.region_9.10_spmd, body=%wide.region_4.9_spmd.sunk | while | flops 418250752 | bytes 23976596 | solution.py:177
  356.2 13.1 fusion.120
  369.4 323.9 %reduce-scatter.6.cloned.1.call-done = f32[1024,1024]{1,0:T(8,128)} async-done(((f32[8192,1024]{1,0:T(8,128)}), f32[1024,1024]{1,0:T(8,128)}) %reduce-scatter.6.cloned.1.call-update) | async-done | bytes 4194320 | tf_op jit(solution)/shard_map/reduce_scatter | solution.py:183
  702.1 147.7 %all-gather.7.cloned.1.call-done = bf16[8192,1024]{1,0:T(8,128)(2,1)} async-done(((bf16[1024,1024]{1,0:T(8,128)(2,1)}), bf16[8192,1024]{1,0:T(8,128)(2,1)}) %all-gather.7.cloned.1.call-update) | async-done | bytes 16777232 | tf_op jit(solution)/shard_map/all_gather | solution.py:198
  849.8 16.3 fusion.121
  866.1 18.1 convolution_convert_fusion.1
  884.2 117.0 %all-gather.9.cloned.1.call-done = bf16[8192,1024]{1,0:T(8,128)(2,1)} async-done(((bf16[1024,1024]{1,0:T(8,128)(2,1)}), bf16[8192,1024]{1,0:T(8,128)(2,1)}) %all-gather.9.cloned.1.call-update) | async-done | bytes 16777232 | tf_op jit(solution)/shard_map/all_gather | solution.py:216
  1001.3 27.1 %convert_reduce_fusion = (f32[512]{0:T(512)}, bf16[8192,512]{1,0:T(8,128)(2,1)}) fusion(f32[8192,512]{1,0:T(8,128)} %fusion.121, f32[512]{0:T(512)S(1)} %convert_element_type.156, bf16[8192,1024]{1,0:T(8,128)(2,1)} %all-gather.9.cloned.1.call-done, bf16[512,1024]{1,0:T(8,128)(2,1)S(1)} %copy-done), kind=kOutput, calls=%fused_computation.111 | convolution fusion | flops 8686403584 | bytes 42995712 | tf_op jit(solution)/shard_map/dot_general | solution.py:46
  1028.4 19.0 fusion.122
  1047.5 122.6 %reduce-scatter.8.cloned.1.call-done = bf16[1024,1024]{1,0:T(8,128)(2,1)} async-done(((bf16[8192,1024]{1,0:T(8,128)(2,1)}), bf16[1024,1024]{1,0:T(8,128)(2,1)}) %reduce-scatter.8.cloned.1.call-update) | async-done | bytes 2097168 | tf_op jit(solution)/shard_map/reduce_scatter | solution.py:204
  1170.1 326.3 %reduce-scatter.10.cloned.1.call-done = f32[1024,1024]{1,0:T(8,128)} async-done(((f32[8192,1024]{1,0:T(8,128)}), f32[1024,1024]{1,0:T(8,128)}) %reduce-scatter.10.cloned.1.call-update) | async-done | bytes 4194320 | tf_op jit(solution)/shard_map/reduce_scatter | solution.py:222
  1496.4 7.6 multiply_reduce_fusion.2
  1505.7 3.2 convert_reduce_fusion.2
  1509.0 149.6 %all-gather.11.cloned.1.call-done = bf16[8192,1024]{1,0:T(8,128)(2,1)} async-done(((bf16[1024,1024]{1,0:T(8,128)(2,1)}), bf16[8192,1024]{1,0:T(8,128)(2,1)}) %all-gather.11.cloned.1.call-update) | async-done | bytes 16777232 | tf_op jit(solution)/shard_map/all_gather | solution.py:237
  1658.6 8.3 convolution_convert_fusion.2
  1666.9 3.3 reshape.647
  1670.2 10.7 copy.66
  1680.9 192.3 %while.36 = (s32[]{:T(128)}, f32[8,1024,2,64]{1,3,2,0:T(8,128)}, bf16[8,1024,2,64]{1,3,2,0:T(8,128)(2,1)}, bf16[8,1024,2,64]{1,3,2,0:T(8,128)(2,1)}, bf16[8,1024...) while((s32[]{:T(128)}, f32[8,1024,2,64]{1,3,2,0:T(8,128)}, ...), condition=%wide.region_23.24_spmd, body=%wide.region_20.23_spmd.sunk | while | flops 1026160640 | bytes 55824564 | solution.py:240
  1693.5 2.9 fusion.192
  1789.5 2.9 fusion.192
  1813.6 2.9 fusion.192
  1876.1 3.7 convert_reduce_fusion.4
  1887.7 13.2 fusion.91
  1900.9 13.2 fusion.94
  1914.1 34.7 %add_add_fusion = f32[8192,1024]{1,0:T(8,128)} fusion(f32[8192,1024]{1,0:T(8,128)} %fusion.94, f32[8192,1024]{1,0:T(8,128)} %fusion.91, bf16[8192,128]{0,1:T(8,128)(2,1)} %bitcast.321, bf16[3,1024,128]{2,1,0:T(8,128)(2,1)S(1)} %copy-done.21), kind=kOutput, calls=%fused_computation.101 | convolution fusion | flops 2164260864 | bytes 103022592 | tf_op jit(solution)/shard_map/dot_general | solution.py:46
  1948.9 17.0 fusion.124
  1965.9 19.4 fusion.112
  1985.4 9.2 fusion.123
  1994.6 8.8 convolution_bitcast_fusion.5
  2003.5 4.6 convolution_bitcast_fusion.7
  2008.1 5.3 convolution_bitcast_fusion.6
  2013.4 259.4 %reduce-scatter.12.cloned.1.call-done = f32[1024,1024]{1,0:T(8,128)} async-done(((f32[8192,1024]{1,0:T(8,128)}), f32[1024,1024]{1,0:T(8,128)}) %reduce-scatter.12.cloned.1.call-update) | async-done | bytes 4194320 | tf_op jit(solution)/shard_map/reduce_scatter | solution.py:272
  2272.8 3.3 fusion.113
  2281.8 13.6 psum.56
  2296.1 6.5 add_add_fusion.3
  2302.6 5.2 reduce-scatter.14.cloned.1.call-done
  2307.8 10.8 all-reduce.2
  2318.5 131.1 %all-reduce.6.cloned.1.call-done = (f32[3,1024,128]{2,1,0:T(8,128)}, f32[128,1024]{1,0:T(8,128)}, f32[1024,512]{1,0:T(8,128)}, f32[512,1024]{1,0:T(8,128)}) async-done(((f32[3,1024,128]{2,1,0:T(8,128)}, f32[128,1024]{1,0:T(8,128)}, f32[1024,512]{1,0:T(8,128)}, f32[512,1024]{1,0:T(8,128)}), (f32[3,1024,128]{2,1,0:T(8,128)}, f32[128,1024]{1,0:T(8,128)}, f32[1024,512]{1,0:T(8,128)}, ...) | async-done | bytes 6291472 | tf_op jit(solution)/shard_map/psum | solution.py:284
  (514 shorter events, 320.6 us)
Async XLA Ops:
  7.2 858.9 %copy-start = (bf16[512,1024]{1,0:T(8,128)(2,1)S(1)}, bf16[512,1024]{1,0:T(8,128)(2,1)}, u32[]{:S(2)}) copy-start(bf16[512,1024]{1,0:T(8,128)(2,1)} %param.33) | copy-start | bytes 3145732
  7.2 5.8 copy-start.4
  7.2 5.1 copy-start.43
  7.2 5.1 copy-start.36
  7.2 161.9 %all-gather.5.cloned.1.call-start = ((), (), s32[]{:S(2)}) async-start(), calls=%async_computation.5 | async-start | bytes 18874368 | tf_op jit(solution)/shard_map/all_gather | solution.py:157
  9.4 5.8 copy-start.44
  9.4 6.2 copy-start.48
  15.1 678.1 %reduce-scatter.6.cloned.1.call-start = ((), (), s32[]{:S(2)}) async-start(), calls=%async_computation.6 | async-start | bytes 37748736 | tf_op jit(solution)/shard_map/reduce_scatter | solution.py:183
  350.6 4.2 copy-start.22
  350.6 5.6 copy-start.23
  369.3 480.4 %all-gather.7.cloned.1.call-start = ((), (), s32[]{:S(2)}) async-start(), calls=%async_computation.7 | async-start | bytes 18874368 | tf_op jit(solution)/shard_map/all_gather | solution.py:198
  700.2 301.1 %all-gather.9.cloned.1.call-start = ((), (), s32[]{:S(2)}) async-start(), calls=%async_computation.9 | async-start | bytes 18874368 | tf_op jit(solution)/shard_map/all_gather | solution.py:216
  700.3 805.4 %copy-start.26 = (f32[1024]{0:T(1024)}, f32[1024]{0:T(1024)S(1)}, u32[]{:S(2)}) copy-start(f32[1024]{0:T(1024)S(1)} %dynamic_slice.64) | copy-start | bytes 12292
  702.0 468.0 %reduce-scatter.8.cloned.1.call-start = ((), (), s32[]{:S(2)}) async-start(), calls=%async_computation.8 | async-start | bytes 18874368 | tf_op jit(solution)/shard_map/reduce_scatter | solution.py:204
  702.1 299.2 %copy-start.46 = (f32[512]{0:T(512)}, f32[512]{0:T(512)S(1)}, u32[]{:S(2)}) copy-start(f32[512]{0:T(512)S(1)} %convert_element_type.156) | copy-start | bytes 6148
  884.2 612.2 %reduce-scatter.10.cloned.1.call-start = ((), (), s32[]{:S(2)}) async-start(), calls=%async_computation.10 | async-start | bytes 37748736 | tf_op jit(solution)/shard_map/reduce_scatter | solution.py:222
  1001.3 27.1 %copy-start.52 = (bf16[1024,512]{1,0:T(8,128)(2,1)S(1)}, bf16[1024,512]{1,0:T(8,128)(2,1)}, u32[]{:S(2)}) copy-start(bf16[1024,512]{1,0:T(8,128)(2,1)} %param.31) | copy-start | bytes 3145732
  1047.4 449.0 %copy-start.42 = (f32[1,1024]{1,0:T(1,128)S(1)}, f32[1,1024]{1,0:T(1,128)}, u32[]{:S(2)}) copy-start(f32[1,1024]{1,0:T(1,128)} %get-tuple-element.409) | copy-start | bytes 12292
  1047.4 611.2 %all-gather.11.cloned.1.call-start = ((), (), s32[]{:S(2)}) async-start(), calls=%async_computation.11 | async-start | bytes 18874368 | tf_op jit(solution)/shard_map/all_gather | solution.py:237
  1496.4 7.6 copy-start.3
  1496.4 7.6 copy-start.11
  1509.0 763.8 %reduce-scatter.12.cloned.1.call-start = ((), (), s32[]{:S(2)}) async-start(), calls=%async_computation.12 | async-start | bytes 37748736 | tf_op jit(solution)/shard_map/reduce_scatter | solution.py:272
  1885.1 15.8 copy-start.12
  1887.7 13.2 copy-start.14
  1948.9 17.1 copy-start.47
  1948.9 358.9 %reduce-scatter.14.cloned.1.call-start = ((), (), s32[]{:S(2)}) async-start(), calls=%async_computation.13 | async-start | bytes 36864 | tf_op jit(solution)/shard_map/reduce_scatter | solution.py:283
  1965.9 19.4 copy-start.10
  1985.4 9.3 copy-start.16
  1985.4 18.0 slice-start
  1985.4 18.0 slice-start.1
  1985.4 18.0 slice-start.2
  1994.6 8.8 copy-start.13
  1994.6 8.8 slice-start.3
  2003.5 4.6 copy-start.15
  2008.1 264.7 %copy-start.5 = (bf16[1024,1024]{1,0:T(8,128)(2,1)S(1)}, bf16[1024,1024]{1,0:T(8,128)(2,1)}, u32[]{:S(2)}) copy-start(bf16[1024,1024]{1,0:T(8,128)(2,1)} %param.27) | copy-start | bytes 6291460
  2008.1 264.7 %copy-start.25 = (f32[1024]{0:T(1024)S(1)}, f32[1024]{0:T(1024)}, u32[]{:S(2)}) copy-start(f32[1024]{0:T(1024)} %copy-done.24) | copy-start | bytes 12292
  2008.1 264.7 %copy-start.29 = (f32[1,1024]{1,0:T(1,128)S(1)}, f32[1,1024]{1,0:T(1,128)}, u32[]{:S(2)}) copy-start(f32[1,1024]{1,0:T(1,128)} %copy-done.28) | copy-start | bytes 12292
  2013.4 262.8 %copy-start.35 = (f32[1024]{0:T(1024)S(1)}, f32[1024]{0:T(1024)}, u32[]{:S(2)}) copy-start(f32[1024]{0:T(1024)} %copy-done.34) | copy-start | bytes 12292
  2013.4 262.8 %copy-start.31 = (f32[1024]{0:T(1024)S(1)}, f32[1024]{0:T(1024)}, u32[]{:S(2)}) copy-start(f32[1024]{0:T(1024)} %copy-done.30) | copy-start | bytes 12292
  2279.2 16.7 copy-start.50
  2279.2 16.7 copy-start.49
  2279.3 16.8 copy-start.27
  2279.3 16.8 copy-start.33
  2279.3 170.3 %all-reduce.6.cloned.1.call-start = ((), (), s32[]{:S(2)}) async-start(), calls=%async_computation.14 | async-start | bytes 12582912 | tf_op jit(solution)/shard_map/psum | solution.py:284
  2296.1 11.7 copy-start.45
  2449.6 4.8 copy-start.19
  2449.6 6.1 copy-start.18
  2452.4 4.6 copy-start.1
  (19 other events, 42.8 us)
Sparse Core Ops, SparseCore 0:
  15.2 153.7 all-gather.4
  369.5 323.7 reduce-scatter.5
  700.3 149.4 all-gather.6
  851.9 149.3 all-gather.8
  1003.6 166.4 reduce-scatter.7
  1172.4 323.8 reduce-scatter.9
  1509.1 149.4 all-gather.10
  1949.0 323.7 reduce-scatter.11
  2279.3 28.3 reduce-scatter.13
  2311.9 137.6 all-reduce.5
where the time goes:
time: 2470 us; the launch traced here: 2460 us
  waiting for transfers between devices  1740 us (70%)
  matrix products  466 us (19%)
  local copies, waits for them, and re-layouts  118 us (5%)
  other arithmetic  103 us (4%)
    reduce_scatter x1, waiting for transfers between devices, body(): lax.psum_scatter(times_back(row_slice(hidden_grad, jnp.int32(0), share *...  326 us
    reduce_scatter x1, waiting for transfers between devices, body(): lax.psum_scatter(jnp.dot(row_slice(attended, jnp.int32(0), share * lax.ax...  324 us
    reduce_scatter x1, waiting for transfers between devices, body(): lax.psum_scatter(total + times_back(row_slice(value_grad, start, share *...  259 us
    all_gather x1, waiting for transfers between devices, body(): attn_rows = lax.all_gather(normed, 'mp', axis=0, tiled=True)  154 us
    all_gather x1, waiting for transfers between devices, body(): branch_use = lax.all_gather(branch_grad, 'mp', axis=0, tiled=True)  150 us
    all_gather x1, waiting for transfers between devices, body(): normed_two_all = lax.all_gather(normed_two, 'mp', axis=0, tiled=True)  148 us
    psum x1, waiting for transfers between devices, body(): lax.psum((qkv_grad, qv_bias_grad, out_grad, up_grad, up_bias_grad, down_g...  131 us
    reduce_scatter x1, waiting for transfers between devices, body(): lax.psum_scatter(jnp.dot(row_slice(active, jnp.int32(0), share * lax.axis...  123 us
  transfers between devices with their start and end apart: 10, of which 10 were waited for; matrix products, arithmetic and copies ran while one was open for 6% of the time, Pallas kernels for 0%

commit v1 on v0

v1 whole, which is shorter than its diff:
```python
import functools
import math

import jax
import jax.numpy as jnp
from jax import lax
from jax.experimental import pallas as pl
from jax.experimental.pallas import tpu as pltpu
from jax.sharding import PartitionSpec as P

HD = 64
PAIR = 128
PART = 32
PIECE = 112
TILE = 256
SLOTS = 1024
DOCS = 6
EPSILON = 1e-05
MASKED = -1e30
LOG2E = math.log2(math.e)
F32, BF16 = jnp.float32, jnp.bfloat16
NN = (((1,), (0,)), ((), ()))
NT = (((1,), (1,)), ((), ()))
TN = (((0,), (0,)), ((), ()))


def mm(a, b, dims):
    return lax.dot_general(a, b, dims, preferred_element_type=F32)


def whole(shape):
    return pl.BlockSpec(shape, lambda *_: (0,) * len(shape), pipeline_mode=pl.Buffered(1))


def call(kernel, grid, ins, outs, scratch=(), gflop=1.0, name=None):
    nbytes = sum(a.size * a.dtype.itemsize for a, _ in ins)
    nbytes += sum(math.prod(s) * jnp.dtype(d).itemsize for s, d, _ in outs)
    return pl.pallas_call(
        kernel,
        grid=grid,
        in_specs=[s for _, s in ins],
        out_specs=[s for _, _, s in outs],
        out_shape=[jax.ShapeDtypeStruct(s, d) for s, d, _ in outs],
        scratch_shapes=list(scratch),
        compiler_params=pltpu.CompilerParams(vmem_limit_bytes=56 << 20),
        cost_estimate=pl.CostEstimate(flops=int(gflop * 1e9), bytes_accessed=nbytes, transcendentals=0),
        name=name,
    )(*[a for a, _ in ins])


def prep_kernel(x_ref, cot_ref, live_ref, gain_ref, shift_ref, h_ref, gf_ref):
    v = x_ref[...].astype(F32)
    spread = v - jnp.mean(v, axis=1, keepdims=True)
    var = jnp.mean(spread * spread, axis=1, keepdims=True)
    h = spread * lax.rsqrt(var + EPSILON) * gain_ref[0:1, :] + shift_ref[0:1, :]
    h_ref[...] = h.astype(BF16)
    gf_ref[...] = (cot_ref[...].astype(F32) * live_ref[...]).astype(BF16)


def prep(x, cot, live, gains, shifts):
    n, d = x.shape
    rows = pl.BlockSpec((TILE, d), lambda i: (i, 0))
    return call(
        prep_kernel, (n // TILE,),
        [(x, rows), (cot, rows), (live, pl.BlockSpec((TILE, 1), lambda i: (i, 0))), (gains, whole(gains.shape)), (shifts, whole(shifts.shape))],
        [((n, d), BF16, rows), ((n, d), BF16, rows)], gflop=1.0, name="prep",
    )


def fill_mask(bias_ref, col_ref, row_ref, transposed):
    n = col_ref.shape[0]
    for i in range(n // TILE):
        part, upto = slice(i * TILE, (i + 1) * TILE), (i + 1) * TILE
        if transposed:
            same = col_ref[:upto, :] == row_ref[:, part]
            key = lax.broadcasted_iota(jnp.int32, (upto, TILE), 0)
            query = lax.broadcasted_iota(jnp.int32, (upto, TILE), 1) + i * TILE
            bias_ref[:upto, part] = jnp.where(same & (key <= query), 0.0, MASKED)
        else:
            same = col_ref[part, :] == row_ref[:, :upto]
            query = lax.broadcasted_iota(jnp.int32, (TILE, upto), 0) + i * TILE
            key = lax.broadcasted_iota(jnp.int32, (TILE, upto), 1)
            bias_ref[part, :upto] = jnp.where(same & (key <= query), 0.0, MASKED)


def pair_rows(w_ref, at):
    return jnp.concatenate([w_ref[j, 0, at : at + PART, :] for j in range(4)], axis=0)


def pair_bias(w_ref, at):
    lane = lax.broadcasted_iota(jnp.int32, (1, PAIR), 1) // PART
    row = jnp.zeros((1, PAIR), F32)
    for j in range(4):
        mine = w_ref[j, 0, 96:112, at : at + PAIR].astype(F32)[0:1, :]
        row = jnp.where(lane == j, mine, row)
    return row


def attend_kernel(col_ref, row_ref, h_ref, w_ref, q_ref, k_ref, v_ref, o_ref, lse_ref, bias_ref):
    n = h_ref.shape[0]

    @pl.when(pl.program_id(0) == 0)
    def _():
        fill_mask(bias_ref, col_ref, row_ref, False)

    wall = jnp.concatenate([pair_rows(w_ref, i * PART) for i in range(3)], axis=0)
    qkv = mm(h_ref[...], wall, NT)
    q_ref[...] = ((qkv[:, :PAIR] + pair_bias(w_ref, 128)) * HD**-0.5).astype(BF16)
    k_ref[...] = qkv[:, PAIR : 2 * PAIR].astype(BF16)
    v = (qkv[:, 2 * PAIR :] + pair_bias(w_ref, 256)).astype(BF16)
    v_ref[...] = v
    vx = jnp.concatenate([v, jnp.ones((n, PAIR), BF16)], axis=1)
    first = lax.broadcasted_iota(jnp.int32, (1, PAIR), 1) < HD
    zero = jnp.zeros((), BF16)
    for i in range(n // TILE):
        part, upto = slice(i * TILE, (i + 1) * TILE), (i + 1) * TILE
        q = q_ref[part, :]
        outs = []
        for h in range(2):
            mine = jnp.where(first, q, zero) if h == 0 else jnp.where(first, zero, q)
            s = mm(mine, k_ref[:upto, :], NT) + bias_ref[part, :upto]
            top = jnp.max(s, axis=1, keepdims=True)
            e = jnp.exp2((s - top) * LOG2E).astype(BF16)
            ov = mm(e, vx[:upto], NN)
            total = ov[:, PAIR:]
            outs.append(ov[:, :PAIR] / total)
            lse_ref[0, h : h + 1, part] = jnp.transpose(top + jnp.log(total))[0:1, :]
        o_ref[part, :] = jnp.where(first, outs[0], outs[1]).astype(BF16)


def attend(col, row, h, w, base=0, pairs=4):
    n, d = h.shape
    blk = pl.BlockSpec((n, PAIR), lambda p: (0, p))
    act = ((n, pairs * PAIR), BF16, blk)
    return call(
        attend_kernel, (pairs,),
        [(col, whole(col.shape)), (row, whole(row.shape)), (h, whole(h.shape)), (w, pl.BlockSpec((4, 1, PIECE, d), lambda p: (0, p + base, 0, 0)))],
        [act, act, act, act, ((pairs, 2, n), F32, pl.BlockSpec((1, 2, n), lambda p: (p, 0, 0)))],
        [pltpu.VMEM((n, n), F32)], gflop=4.0 * pairs, name="attend",
    )


def join_kernel(*refs):
    x_ref, o_refs, (wa_ref, wb_ref, gain_ref, shift_ref, r_ref, h_ref, wo_ref) = refs[0], refs[1:-7], refs[-7:]

    @pl.when(pl.program_id(0) == 0)
    def _():
        for half, w_ref in enumerate((wa_ref, wb_ref)):
            for z in range(4):
                for j in range(4):
                    lo = (half * 4 + z) * PAIR + j * PART
                    wo_ref[lo : lo + PART, :] = w_ref[j, z, :, :]

    branch, lo = shift_ref[1:2, :], 0
    for o_ref in o_refs:
        hi = lo + o_ref.shape[1]
        branch = branch + mm(o_ref[...], wo_ref[lo:hi, :], NN)
        lo = hi
    r = x_ref[...].astype(F32) + branch
    r_ref[...] = r
    spread = r - jnp.mean(r, axis=1, keepdims=True)
    var = jnp.mean(spread * spread, axis=1, keepdims=True)
    h_ref[...] = (spread * lax.rsqrt(var + EPSILON) * gain_ref[1:2, :] + shift_ref[2:3, :]).astype(BF16)


def join(x, os, wa, wb, gains, shifts):
    n, d = x.shape
    rows = pl.BlockSpec((TILE, d), lambda i: (i, 0))
    out = pl.BlockSpec((4, 4, PART, d), lambda i: (0, 0, PAIR // PART, 0), pipeline_mode=pl.Buffered(1))
    return call(
        join_kernel, (n // TILE,),
        [(x, rows)] + [(o, pl.BlockSpec((TILE, o.shape[1]), lambda i: (i, 0))) for o in os]
        + [(wa, out), (wb, out), (gains, whole(gains.shape)), (shifts, whole(shifts.shape))],
        [((n, d), F32, rows), ((n, d), BF16, rows)],
        [pltpu.VMEM((d, d), BF16)], gflop=4.0, name="join",
    )


UNITS = 512


def up_kernel(h_ref, w_ref, b_ref, act_ref, slope_ref):
    u = mm(h_ref[...], w_ref[0].reshape(UNITS, -1), NT) + b_ref[...].astype(F32)
    c0, c1 = math.sqrt(2 / math.pi), math.sqrt(2 / math.pi) * 0.044715
    square = u * u
    t = jnp.tanh(u * (c0 + c1 * square))
    half = 0.5 + 0.5 * t
    act_ref[...] = (u * half).astype(BF16)
    slope_ref[...] = (half + u * (0.5 - 0.5 * t * t) * (c0 + 3 * c1 * square)).astype(BF16)


def up(h, w, b):
    n, d = h.shape
    blk = pl.BlockSpec((n, UNITS), lambda i: (0, i))
    shape = (n, 4 * UNITS)
    return call(
        up_kernel, (4,),
        [(h, whole(h.shape)), (w, pl.BlockSpec((1, 4, PAIR, d), lambda i: (i, 0, 0, 0))), (b, pl.BlockSpec((1, UNITS), lambda i: (0, i)))],
        [(shape, BF16, blk), (shape, BF16, blk)], gflop=6.0, name="up",
    )


def down_kernel(aa_ref, ab_ref, wa_ref, wb_ref, r_ref, gf_ref, shift_ref, mixed_ref, loss_ref, acc_ref):
    t, last = pl.program_id(0), pl.num_programs(0) - 1
    half = pl.num_programs(0) // 2

    @pl.when(t == 0)
    def _():
        acc_ref[...] = mm(aa_ref[...], wa_ref[...], NN)

    @pl.when((t > 0) & (t < half))
    def _():
        acc_ref[...] += mm(aa_ref[...], wa_ref[...], NN)

    @pl.when(t >= half)
    def _():
        acc_ref[...] += mm(ab_ref[...], wb_ref[...], NN)

    @pl.when(t == last)
    def _():
        out = r_ref[...] + (acc_ref[...] + shift_ref[3:4, :])
        mixed_ref[...] = out.astype(BF16)
        loss = jnp.sum(out * gf_ref[...].astype(F32), axis=0, keepdims=True)
        loss_ref[...] = jnp.broadcast_to(jnp.sum(loss, axis=1, keepdims=True), loss_ref.shape)


def own(shape, steps, axis):
    at = lambda t: jnp.minimum(t, steps - 1)
    return pl.BlockSpec(shape, (lambda t: (at(t), 0)) if axis == 0 else (lambda t: (0, at(t))))


def oth(shape, steps, axis):
    at = lambda t: jnp.maximum(t - steps, 0)
    return pl.BlockSpec(shape, (lambda t: (at(t), 0)) if axis == 0 else (lambda t: (0, at(t))))


def down(aa, ab, wa, wb, r, gf, shifts):
    n, d = r.shape
    steps = wa.shape[0] // UNITS
    return call(
        down_kernel, (2 * steps,),
        [(aa, own((n, UNITS), steps, 1)), (ab, oth((n, UNITS), steps, 1)), (wa, own((UNITS, d), steps, 0)), (wb, oth((UNITS, d), steps, 0)),
         (r, whole(r.shape)), (gf, whole(gf.shape)), (shifts, whole(shifts.shape))],
        [((n, d), BF16, whole((n, d))), ((8, 128), F32, whole((8, 128)))],
        [pltpu.VMEM((n, d), F32)], gflop=9.0, name="down",
    )


def back_kernel(gf_ref, sa_ref, sb_ref, da_ref, db_ref, ua_ref, ub_ref, r_ref, gain_ref, ga_out, gb_out, gr_ref, br_ref, vec_ref, acc_ref):
    t, last = pl.program_id(0), pl.num_programs(0) - 1
    half = pl.num_programs(0) // 2

    @pl.when(t < half)
    def _():
        g = (mm(gf_ref[...], da_ref[...], NT) * sa_ref[...].astype(F32)).astype(BF16)
        ga_out[...] = g
        part = mm(g, ua_ref[0].reshape(UNITS, -1), NN)

        @pl.when(t == 0)
        def _():
            acc_ref[...] = part

        @pl.when(t > 0)
        def _():
            acc_ref[...] += part

    @pl.when(t >= half)
    def _():
        g = (mm(gf_ref[...], db_ref[...], NT) * sb_ref[...].astype(F32)).astype(BF16)
        gb_out[...] = g
        acc_ref[...] += mm(g, ub_ref[0].reshape(UNITS, -1), NN)

    @pl.when(t == last)
    def _():
        n, d = r_ref.shape
        sums = [jnp.zeros((1, d), F32) for _ in range(4)]
        for i in range(n // TILE):
            part = slice(i * TILE, (i + 1) * TILE)
            r, gy, c = r_ref[part, :], acc_ref[part, :], gf_ref[part, :].astype(F32)
            spread = r - jnp.mean(r, axis=1, keepdims=True)
            rstd = lax.rsqrt(jnp.mean(spread * spread, axis=1, keepdims=True) + EPSILON)
            norm = spread * rstd
            gn = gy * gain_ref[1:2, :]
            gv = rstd * (gn - jnp.mean(gn, axis=1, keepdims=True) - norm * jnp.mean(gn * norm, axis=1, keepdims=True))
            gr = c + gv
            gr_ref[part, :] = gr
            branch = gr.astype(BF16)
            br_ref[part, :] = branch
            for at, value in enumerate((gy * norm, gy, branch.astype(F32), c)):
                sums[at] += jnp.sum(value, axis=0, keepdims=True)
        vec_ref[...] = jnp.concatenate(sums + [jnp.zeros((4, d), F32)], axis=0)


def back(gf, sa, sb, da, db, ua, ub, r, gains):
    n, d = r.shape
    steps = da.shape[0] // UNITS
    wa, wb = own((UNITS, d), steps, 0), oth((UNITS, d), steps, 0)
    ta, tb = own((n, UNITS), steps, 1), oth((n, UNITS), steps, 1)
    pa = pl.BlockSpec((1, 4, PAIR, d), lambda t: (jnp.minimum(t, steps - 1), 0, 0, 0))
    pb = pl.BlockSpec((1, 4, PAIR, d), lambda t: (jnp.maximum(t - steps, 0), 0, 0, 0))
    return call(
        back_kernel, (2 * steps,),
        [(gf, whole(gf.shape)), (sa, ta), (sb, tb), (da, wa), (db, wb), (ua, pa), (ub, pb), (r, whole(r.shape)), (gains, whole(gains.shape))],
        [(sa.shape, BF16, ta), (sb.shape, BF16, tb), ((n, d), F32, whole((n, d))), ((n, d), BF16, whole((n, d))), ((8, d), F32, whole((8, d)))],
        [pltpu.VMEM((n, d), F32)], gflop=19.0, name="back",
    )


def halves(rows):
    return rows // 2 // 16 * 16


def outer_kernel(la_ref, lb_ref, ra_ref, rb_ref, *outs):
    g = (mm(la_ref[...], ra_ref[...], TN) + mm(lb_ref[...], rb_ref[...], TN)).astype(BF16)
    t = pl.program_id(0)
    for j in range(3):

        @pl.when(t == j)
        def _():
            outs[j][...] = g

    @pl.when(t == 3)
    def _():
        cut = outs[3].shape[0]
        outs[3][...] = g[:cut]
        outs[4][...] = g[cut:]

    outs[5][...] = jnp.sum(la_ref[...].astype(F32) + lb_ref[...].astype(F32), axis=0, keepdims=True)


def outer(la, lb, ra, rb):
    n, m = la.shape
    d = ra.shape[1]
    tile = pl.BlockSpec((n, UNITS), lambda i: (0, i))
    cut = halves(UNITS)
    rows = (UNITS, UNITS, UNITS, cut, UNITS - cut)
    *g, total = call(
        outer_kernel, (4,),
        [(la, tile), (lb, tile), (ra, whole(ra.shape)), (rb, whole(rb.shape))],
        [((k, d), BF16, whole((k, d))) for k in rows] + [((1, m), F32, pl.BlockSpec((1, UNITS), lambda i: (0, i)))],
        gflop=9.0, name="outer",
    )
    return g, total


def attend_back_kernel(col_ref, row_ref, ga_ref, wo_ref, q_ref, k_ref, v_ref, o_ref, lse_ref, gq_ref, gk_ref, gv_ref, bias_ref, ka_ref, va_ref, go_ref):
    n = q_ref.shape[0]

    @pl.when(pl.program_id(0) == 0)
    def _():
        fill_mask(bias_ref, col_ref, row_ref, True)

    w = jnp.concatenate([wo_ref[j, 0, :, :] for j in range(4)], axis=0)
    go_ref[...] = mm(ga_ref[...], w, NT).astype(BF16)
    first = lax.broadcasted_iota(jnp.int32, (1, PAIR), 1) < HD
    zero = jnp.zeros((), BF16)
    split = lambda a: (jnp.where(first, a, zero), jnp.where(first, zero, a))
    ks = split(k_ref[...])
    for i in range(n // TILE):
        part, upto = slice(i * TILE, (i + 1) * TILE), (i + 1) * TILE
        qs, gs = split(q_ref[part, :]), split(go_ref[part, :])
        prod = jnp.transpose(go_ref[part, :].astype(F32) * o_ref[part, :].astype(F32))
        ps, ds = [], []
        for h in range(2):
            delta = jnp.sum(prod[h * HD : (h + 1) * HD, :], axis=0, keepdims=True)
            s = mm(k_ref[:upto, :], qs[h], NT) + bias_ref[:upto, part]
            p = jnp.exp2((s - lse_ref[0, h : h + 1, part]) * LOG2E)
            dp = mm(v_ref[:upto, :], gs[h], NT)
            ds.append((p * (dp - delta)).astype(BF16))
            ps.append(p.astype(BF16))
        gv = mm(jnp.concatenate(ps, 1), jnp.concatenate(gs, 0), NN)
        gk = mm(jnp.concatenate(ds, 1), jnp.concatenate(qs, 0), NN)
        gq = mm(ds[0], ks[0][:upto], TN) + mm(ds[1], ks[1][:upto], TN)
        gq_ref[part, :] = (gq.astype(BF16).astype(F32) * HD**-0.5).astype(BF16)
        lo = i * TILE
        if i:
            va_ref[:lo, :] += gv[:lo]
            ka_ref[:lo, :] += gk[:lo]
        va_ref[part, :] = gv[lo:]
        ka_ref[part, :] = gk[lo:]
    gk_ref[...] = ka_ref[...].astype(BF16)
    gv_ref[...] = va_ref[...].astype(BF16)


def attend_back(col, row, ga, wo, base, q, k, v, o, lse):
    n, d = ga.shape
    pairs = lse.shape[0]
    blk = pl.BlockSpec((n, PAIR), lambda p: (0, p))
    act = ((n, pairs * PAIR), BF16, blk)
    return call(
        attend_back_kernel, (pairs,),
        [(col, whole(col.shape)), (row, whole(row.shape)), (ga, whole(ga.shape)), (wo, pl.BlockSpec((4, 1, PART, d), lambda p: (0, p + base, PAIR // PART, 0))),
         (q, blk), (k, blk), (v, blk), (o, blk), (lse, pl.BlockSpec((1, 2, n), lambda p: (p, 0, 0)))],
        [act, act, act],
        [pltpu.VMEM((n, n), F32), pltpu.VMEM((n, PAIR), F32), pltpu.VMEM((n, PAIR), F32), pltpu.VMEM((n, PAIR), BF16)],
        gflop=5.0 * pairs, name="attend_back",
    )


ATTN = PIECE + PART


def outer_attn_kernel(qa_ref, qb_ref, ka_ref, kb_ref, va_ref, vb_ref, oa_ref, ob_ref, ha_ref, hb_ref, ga_ref, gb_ref, up_ref, *outs):
    p, pairs = pl.program_id(0), pl.num_programs(0)
    rows = []
    for a_ref, b_ref, c_ref, d_ref in ((qa_ref, qb_ref, ha_ref, hb_ref), (ka_ref, kb_ref, ha_ref, hb_ref), (va_ref, vb_ref, ha_ref, hb_ref), (oa_ref, ob_ref, ga_ref, gb_ref)):
        rows.append((mm(a_ref[...], c_ref[...], TN) + mm(b_ref[...], d_ref[...], TN)).astype(BF16))
    total = lambda a_ref, b_ref: jnp.sum(a_ref[...].astype(F32) + b_ref[...].astype(F32), axis=0, keepdims=True)
    qsum, vsum = total(qa_ref, qb_ref), total(va_ref, vb_ref)
    d = ha_ref.shape[1]
    for j in range(4):
        turn = lambda a: jnp.concatenate([a[:, j * PART :], a[:, : j * PART]], axis=1) if j else a
        line = jnp.concatenate([up_ref[j, 0, 0:1, :], turn(qsum), turn(vsum), jnp.zeros((1, d - 3 * PAIR), F32)], axis=1)
        line = jnp.concatenate([line, jnp.zeros((15, d), F32)], axis=0).astype(BF16)
        part = [rows[i][j * PART : (j + 1) * PART, :] for i in range(4)]
        outs[j][...] = jnp.concatenate(part[:3] + [line] + part[3:], axis=0)


def outer_attn(qs, ks, vs, os, hs, gs, upsum):
    n, m = qs[0].shape
    d = hs[0].shape[1]
    pairs = m // PAIR
    tile = pl.BlockSpec((n, PAIR), lambda p: (0, p))
    return call(
        outer_attn_kernel, (pairs,),
        [(a, tile) for a in (*qs, *ks, *vs, *os)] + [(a, whole(a.shape)) for a in (*hs, *gs)]
        + [(upsum, pl.BlockSpec((4, 1, 8, PAIR), lambda p: (0, p, 0, 0)))],
        [((pairs * ATTN, d), BF16, pl.BlockSpec((ATTN, d), lambda p: (p, 0)))] * 4,
        gflop=2.5 * pairs, name="outer_attn",
    )


def finish_kernel(*refs, spans):
    grads, (wa_ref, wb_ref, x_ref, gr_ref, gain_ref, out_ref, vec_ref, acc_ref) = refs[:-8], refs[-8:]
    t, last = pl.program_id(0), pl.num_programs(0) - 1
    for at, (lo, hi, half) in enumerate(spans):

        @pl.when((t >= lo) & (t < hi))
        def _():
            w_ref = wb_ref if half else wa_ref
            wall = jnp.concatenate([pair_rows(w_ref, i * PART) for i in range(3)], axis=0)
            part = mm(jnp.concatenate([ref[...] for ref in grads[3 * at : 3 * at + 3]], axis=1), wall, NN)
            if lo == 0:
                acc_ref[...] = jnp.where(t == 0, part, acc_ref[...] + part)
            else:
                acc_ref[...] += part

    @pl.when(t == last)
    def _():
        n, d = x_ref.shape
        sums = [jnp.zeros((1, d), F32) for _ in range(2)]
        for i in range(n // TILE):
            rows = slice(i * TILE, (i + 1) * TILE)
            x, gy = x_ref[rows, :].astype(F32), acc_ref[rows, :]
            spread = x - jnp.mean(x, axis=1, keepdims=True)
            rstd = lax.rsqrt(jnp.mean(spread * spread, axis=1, keepdims=True) + EPSILON)
            norm = spread * rstd
            gn = gy * gain_ref[0:1, :]
            gv = rstd * (gn - jnp.mean(gn, axis=1, keepdims=True) - norm * jnp.mean(gn * norm, axis=1, keepdims=True))
            out_ref[rows, :] = gr_ref[rows, :] + gv
            for at, value in enumerate((gy * norm, gy)):
                sums[at] += jnp.sum(value, axis=0, keepdims=True)
        vec_ref[...] = jnp.concatenate(sums + [jnp.zeros((6, d), F32)], axis=0)


def finish(grads, wa, wb, x, gr, gains):
    n, d = x.shape
    ins, spans, lo = [], [], 0
    firsts = {0: [], 1: []}
    for gq, gk, gv, base, half in grads:
        count = gq.shape[1] // PAIR
        spec = pl.BlockSpec((n, PAIR), lambda t, lo=lo, count=count: (0, jnp.clip(t - lo, 0, count - 1)))
        ins += [(gq, spec), (gk, spec), (gv, spec)]
        spans.append((lo, lo + count, half))
        firsts[half].append((lo, base))
        lo += count

    def pick(half):
        def at(t):
            pair = firsts[half][0][1]
            for lo, hi, which in spans:
                if which == half:
                    base = dict(firsts[half])[lo]
                    pair = jnp.where(t >= lo, base + jnp.minimum(t - lo, hi - lo - 1), pair)
            return (0, pair, 0, 0)

        return pl.BlockSpec((4, 1, PIECE, d), at)

    return call(
        functools.partial(finish_kernel, spans=spans), (lo,),
        ins + [(wa, pick(0)), (wb, pick(1)), (x, whole(x.shape)), (gr, whole(gr.shape)), (gains, whole(gains.shape))],
        [((n, d), F32, whole((n, d))), ((8, d), F32, whole((8, d)))],
        [pltpu.VMEM((n, d), F32)], gflop=10.0, name="finish",
    )


def pack_kernel(r_ref, *refs, plan, bands):
    srcs, (out_ref, held_ref, in_sem, out_sem) = refs[:-4], refs[-4:]
    copies = []
    for at, (src, quarter, count, dst) in enumerate(plan):
        source = srcs[src] if quarter is None else srcs[src].at[r_ref[0] ^ quarter]
        copies.append(pltpu.make_async_copy(source, held_ref.at[pl.ds(dst, count)], in_sem.at[at]))
    for copy in copies:
        copy.start()
    band = held_ref.shape[0] // bands
    outs = []
    for b in range(bands):
        for copy, (_, _, _, dst) in zip(copies, plan):
            if dst // band == b:
                copy.wait()
        span = pl.ds(b * band, band)
        outs.append(pltpu.make_async_copy(held_ref.at[span], out_ref.at[span], out_sem.at[b]))
        outs[-1].start()
    for out in outs:
        out.wait()


def pack(r, arrays, plan, bands=1):
    rows = sum(count for _, _, count, _ in plan)
    d = arrays[0].shape[-1]
    anywhere = pl.BlockSpec(memory_space=pl.ANY)
    return pl.pallas_call(
        functools.partial(pack_kernel, plan=plan, bands=bands),
        in_specs=[pl.BlockSpec(memory_space=pltpu.SMEM)] + [anywhere] * len(arrays),
        out_specs=anywhere,
        out_shape=jax.ShapeDtypeStruct((rows, d), BF16),
        scratch_shapes=[pltpu.VMEM((rows, d), BF16), pltpu.SemaphoreType.DMA((len(plan),)), pltpu.SemaphoreType.DMA((bands,))],
        compiler_params=pltpu.CompilerParams(vmem_limit_bytes=56 << 20),
        cost_estimate=pl.CostEstimate(flops=0, bytes_accessed=4 * rows * d, transcendentals=0),
        name="pack",
    )(r, *arrays)


def moved(array, axis, mask):
    size = lax.axis_size(axis)
    return lax.ppermute(array, axis, [(i, i ^ mask) for i in range(size)])


def across(array):
    return moved(array, "mp", 1)


def beside_x(a):
    return moved(a, "rows", 1)


def beside_y(a):
    return moved(a, "rows", 2)


def along_z(a, z):
    return moved(a, "mp", 2 * z)


def fence(*trees):
    return lax.optimization_barrier(trees)


def relative(a):
    r = lax.axis_index("rows")
    low = [jnp.where(r & 1, a[i ^ 1], a[i]) for i in range(4)]
    return [jnp.where(r & 2, low[i ^ 2], low[i]) for i in range(4)]


def added(*terms):
    total = terms[0].astype(F32)
    for term in terms[1:]:
        total = total + term.astype(F32)
    return total.astype(BF16)


def stack_z(r, parts):
    n = parts[0].shape[0]
    return pack(r, parts, [(i, None, n, i * n) for i in range(3)])


def stack_all(r, quarters, s, x, y, dx, dy):
    n, cut = quarters.shape[1], dx.shape[0]
    plan = [(0, j, n, 4 * n * j) for j in range(4)]
    plan += [(1, None, 3 * n, n), (2, None, 3 * n, 5 * n), (3, None, 3 * n, 9 * n), (4, None, cut, 13 * n), (5, None, 3 * n - cut, 13 * n + cut)]
    return pack(r, [quarters, s, x, y, dx, dy], plan, 4).reshape(4, 4, n, -1)


def second_hop(g, ax, ay):
    cut = ax.shape[0]
    to_x = jnp.concatenate([g[1][:cut], added(g[1][cut:], ay)], axis=0)
    to_y = jnp.concatenate([added(g[2][:cut], ax), g[2][cut:]], axis=0)
    return to_x, to_y


def shard_of(f, fx, fy, fd):
    return jnp.stack(relative([f, fx, fy, fd])).astype(F32)


def any_spread(parts):
    core = lax.axis_index("mp") % 2
    return [lax.dynamic_index_in_dim(parts, c, 0, False) for c in (core, 1 - core)]


def any_reduced(full, axis):
    return lax.psum(lax.psum_scatter(full, "mp", scatter_dimension=axis, tiled=True), "rows")


def up_biases(w):
    return w[:, :, 96, :PAIR].reshape(1, -1)


def up_sums(total, pairs):
    return jnp.pad(total.reshape(4, 4, 1, PAIR)[:, pairs], ((0, 0), (0, 0), (0, 7), (0, 0)))


def stacked_vectors(one, two, loss):
    d = one.shape[1]
    at = lax.axis_index("rows") * lax.axis_size("mp") + lax.axis_index("mp")
    losses = jnp.where(jnp.arange(d, dtype=jnp.int32) == at, loss[0, 0] / math.sqrt(SLOTS * d), 0.0)
    return jnp.stack([one[0], two[0], one[1], two[2], two[1], two[3], losses, jnp.zeros_like(losses)])


def any_mesh(tokens, qkv_rows, qv_bias, out_weight, up_rows, up_bias, down_weight, gains, shifts, live, col, line, cotangent):
    d = tokens.shape[1]
    every = lambda a, axis=0: lax.all_gather(a, "mp", axis=axis, tiled=True)
    heads = lambda a: a.reshape(2, 4, 4, PART, d).swapaxes(1, 2)
    qkv_all, qvb_all = every(qkv_rows, 1), every(qv_bias, 1)
    small = lambda a: jnp.tile(a.reshape(2, 4, 4, PART).swapaxes(1, 2), (1, 1, 1, 4))
    bias = jnp.concatenate([every(up_bias).reshape(2, 4, 4, PAIR), small(qvb_all[0]), small(qvb_all[1])], axis=3)
    bias = jnp.pad(bias[:, :, :, None, :], ((0, 0), (0, 0), (0, 0), (0, PIECE - 97), (0, d - 3 * PAIR)))
    wa, wb = any_spread(jnp.concatenate([heads(qkv_all[0]), heads(qkv_all[1]), heads(qkv_all[2]), bias], axis=3))
    ua, ub = any_spread(jnp.concatenate([every(up_rows).reshape(2, 4, 4, PAIR, d), heads(every(out_weight))], axis=3))
    da, db = [w.reshape(-1, d) for w in any_spread(every(down_weight).reshape(2, 4, 4, PAIR, d))]
    h1, gf = prep(tokens, cotangent, live, gains, shifts)
    *qkv_a, oa, la = attend(col, line, h1, wa)
    *qkv_b, ob, lb = attend(col, line, h1, wb)
    r, h2 = join(tokens, [oa, ob], ua, ub, gains, shifts)
    aa, sa = up(h2, ua, up_biases(wa))
    ab, sb = up(h2, ub, up_biases(wb))
    g_down, _ = outer(aa, across(ab), gf, across(gf))
    mixed, loss = down(aa, ab, da, db, r, gf, shifts)
    ga, gb, gr, branch, two = back(gf, sa, sb, da, db, ua, ub, r, gains)
    g_up, total = outer(ga, across(gb), h2, across(h2))
    back_b = attend_back(col, line, branch, ub, 0, *qkv_b, ob, lb)
    back_a = attend_back(col, line, branch, ua, 0, *qkv_a, oa, la)
    pairs = [(a, across(b)) for a, b in zip(back_a, back_b)]
    g_attn = outer_attn(*pairs, (oa, across(ob)), (h1, across(h1)), (branch, across(branch)), up_sums(total, slice(0, 4)))
    g_attn = jnp.stack(g_attn).reshape(4, 4, ATTN, d)
    input_grad, one = finish([(*back_a, 0, 0), (*back_b, 0, 1)], wa, wb, tokens, gr, gains)
    vectors = lax.psum(stacked_vectors(one, two, loss), ("rows", "mp"))
    core = lax.axis_index("mp") % 2
    full = lambda g: lax.dynamic_update_index_in_dim(jnp.zeros((2,) + g.shape, F32), g.astype(F32), core, 0)
    down_grad, up_grad = [any_reduced(full(jnp.concatenate(g)).reshape(-1, d), 0) for g in (g_down, g_up)]
    ordered = lambda g: full(g).swapaxes(1, 2).reshape(-1, g.shape[-1])
    out_grad = any_reduced(ordered(g_attn[:, :, PIECE:]), 0)
    qkv_grad = any_reduced(jnp.stack([ordered(g_attn[:, :, i * PART : (i + 1) * PART]) for i in range(3)]), 1)
    up_bias_grad = any_reduced(full(g_attn[:, :, 96, :PAIR]).reshape(-1), 0)
    ordered = lambda g: full(g).swapaxes(1, 2).reshape(-1)
    qv_bias_grad = any_reduced(jnp.stack([ordered(g_attn[:, :, 96, at : at + PART]) for at in (PAIR, 2 * PAIR)]), 1)
    return mixed, input_grad, qkv_grad, qv_bias_grad, out_grad, up_grad, up_bias_grad, down_grad, vectors


def small_mesh(tokens, qkv_rows, qv_bias, out_weight, up_rows, up_bias, down_weight, gains, shifts, live, col, line, cotangent):
    d = tokens.shape[1]
    row = lax.axis_index("rows")
    r = row.reshape(1).astype(jnp.int32)
    mine = lambda a: lax.dynamic_index_in_dim(a, row, 0, False)
    xy = lambda s: (beside_x(s), beside_y(s))
    zs = lambda p, which=(1, 2, 3): [along_z(p, z) for z in which]

    def corner(x, y):
        cut = halves(x.shape[0])
        return beside_x(y[:cut]), beside_y(x[cut:])

    bias = jnp.concatenate(
        [up_bias.reshape(4, PAIR), jnp.tile(qv_bias[0].reshape(4, PART), (1, 4)), jnp.tile(qv_bias[1].reshape(4, PART), (1, 4))], axis=1
    )
    bias = jnp.pad(bias[:, None, :], ((0, 0), (0, PIECE - 97), (0, d - 3 * PAIR)))
    a4 = jnp.concatenate([qkv_rows.reshape(3, 4, PART, d).swapaxes(0, 1).reshape(4, 3 * PART, d), bias], axis=1)
    za = zs(mine(a4))
    b4 = jnp.concatenate([up_rows.reshape(4, PAIR, d), out_weight.reshape(4, PART, d)], axis=1)
    c4 = down_weight.reshape(4, PAIR, d)
    pb, pc = mine(b4), mine(c4)
    h1, gf = prep(tokens, cotangent, live, gains, shifts)
    a0 = pack(r, [a4], [(0, j, PIECE, j * PIECE) for j in range(4)]).reshape(4, 1, PIECE, d)
    *qkv_a0, oa0, la0 = attend(col, line, h1, a0, 0, 1)
    za, b4, c4, pb, pc, h1, gf, oa0 = fence(za, b4, c4, pb, pc, h1, gf, oa0)
    s_a = stack_z(r, za)
    x_a, y_a = xy(s_a)
    zb = zs(pb, (1, 2))
    h1_x, gf_x = across(h1), across(gf)
    x_a, y_a, zb, pb, h1_x, gf_x = fence(x_a, y_a, zb, pb, h1_x, gf_x)
    dx, dy = corner(x_a, y_a)
    zb = zb + zs(pb, (3,))
    dx, dy, zb, pc = fence(dx, dy, zb, pc)
    wa = stack_all(r, a4, s_a, x_a, y_a, dx, dy)
    wb = across(wa)
    s_b = stack_z(r, zb)
    x_b, y_b = xy(s_b)
    zc = zs(pc, (1, 2))
    *qkv_a1, oa1, la1 = attend(col, line, h1, wa, 1, 3)
    wb, x_b, y_b, zc, oa1, pc = fence(wb, x_b, y_b, zc, oa1, pc)
    dx, dy = corner(x_b, y_b)
    zc = zc + zs(pc, (3,))
    *qkv_b1, ob1, lb1 = attend(col, line, h1, wb, 1, 3)
    dx, dy, zc, ob1, wb = fence(dx, dy, zc, ob1, wb)
    ua = stack_all(r, b4, s_b, x_b, y_b, dx, dy)
    ub = across(ua)
    s_c = stack_z(r, zc)
    x_c, y_c = xy(s_c)
    *qkv_b0, ob0, lb0 = attend(col, line, h1, wb, 0, 1)
    res, h2 = join(tokens, [oa0, oa1, ob0, ob1], ua, ub, gains, shifts)
    x_c, y_c, ub, res, h2 = fence(x_c, y_c, ub, res, h2)
    dx, dy = corner(x_c, y_c)
    ab, sb = up(h2, ub, up_biases(wb))
    dx, dy, ab, h2 = fence(dx, dy, ab, h2)
    da = stack_all(r, c4, s_c, x_c, y_c, dx, dy).reshape(-1, d)
    db = across(da)
    ab_x, h2_x = across(ab), across(h2)
    ob0_x, ob1_x = across(ob0), across(ob1)
    aa, sa = up(h2, ua, up_biases(wa))
    db, ab_x, h2_x, ob0_x, ob1_x, aa = fence(db, ab_x, h2_x, ob0_x, ob1_x, aa)
    g, _ = outer(aa, ab_x, gf, gf_x)
    g, db = fence(g, db)
    ax, ay = beside_x(g[3]), beside_y(g[4])
    mixed, loss = down(aa, ab, da, db, res, gf, shifts)
    ax, ay, mixed, loss, db = fence(ax, ay, mixed, loss, db)
    to_x, to_y = second_hop(g, ax, ay)
    fx, fy = beside_x(to_x), beside_y(to_y)
    ga, gb, gr, branch, two = back(gf, sa, sb, da, db, ua, ub, res, gains)
    fx, fy, ga, gb, gr, branch = fence(fx, fy, ga, gb, gr, branch)
    t = added(g[0], fx, fy).reshape(4, PAIR, d)
    zr = [along_z(t[z], z) for z in (1, 2, 3)]
    gb_x, branch_x = across(gb), across(branch)
    back_b1 = attend_back(col, line, branch, ub, 1, *qkv_b1, ob1, lb1)
    zr, gb_x, branch_x, back_b1 = fence(zr, gb_x, branch_x, back_b1)
    f = added(t[0], *zr)
    fx, fy = beside_x(f), beside_y(f)
    back_b1_x = [across(a) for a in back_b1]
    g, total = outer(ga, gb_x, h2, h2_x)
    fx, fy, back_b1_x, g, branch = fence(fx, fy, back_b1_x, g, branch)
    ax, ay, fd = beside_x(g[3]), beside_y(g[4]), beside_x(fy)
    back_a1 = attend_back(col, line, branch, ua, 1, *qkv_a1, oa1, la1)
    ax, ay, fd, back_a1, h1 = fence(ax, ay, fd, back_a1, h1)
    down_grad = shard_of(f, fx, fy, fd).reshape(-1, d)
    to_x, to_y = second_hop(g, ax, ay)
    fx, fy = beside_x(to_x), beside_y(to_y)
    pairs = list(zip(back_a1, back_b1_x))
    n1 = outer_attn(*pairs, (oa1, ob1_x), (h1, h1_x), (branch, branch_x), up_sums(total, slice(1, 4)))
    back_b0 = attend_back(col, line, branch, ub, 0, *qkv_b0, ob0, lb0)
    fx, fy, n1, back_b0, branch = fence(fx, fy, n1, back_b0, branch)
    t = added(g[0], fx, fy).reshape(4, PAIR, d)
    zr = [along_z(t[z], z) for z in (1, 2, 3)]
    cut = halves(n1[3].shape[0])
    ax, ay = beside_x(n1[3][:cut]), beside_y(n1[3][cut:])
    back_b0_x = [across(a) for a in back_b0]
    back_a0 = attend_back(col, line, branch, ua, 0, *qkv_a0, oa0, la0)
    zr, ax, ay, back_b0_x, back_a0, h1 = fence(zr, ax, ay, back_b0_x, back_a0, h1)
    f = added(t[0], *zr)
    fx, fy = beside_x(f), beside_y(f)
    to_x, to_y = second_hop(n1, ax, ay)
    ex, ey = beside_x(to_x), beside_y(to_y)
    pairs = list(zip(back_a0, back_b0_x))
    n0 = outer_attn(*pairs, (oa0, ob0_x), (h1, h1_x), (branch, branch_x), up_sums(total, slice(0, 1)))
    fx, fy, ex, ey, n0, wa = fence(fx, fy, ex, ey, n0, wa)
    fd = beside_x(fy)
    t = added(n1[0], ex, ey).reshape(3, ATTN, d)
    zr = [along_z(t[z - 1], z) for z in (1, 2, 3)]
    cut = halves(n0[3].shape[0])
    ax, ay = beside_x(n0[3][:cut]), beside_y(n0[3][cut:])
    grads = [(*back_a0, 0, 0), (*back_a1, 1, 0), (*back_b0, 0, 1), (*back_b1, 1, 1)]
    input_grad, one = finish(grads, wa, wb, tokens, gr, gains)
    fd, zr, ax, ay, input_grad, one = fence(fd, zr, ax, ay, input_grad, one)
    to_x, to_y = second_hop(n0, ax, ay)
    ex, ey = beside_x(to_x), beside_y(to_y)
    vectors = stacked_vectors(one, two, loss)
    vx = beside_x(vectors)
    up_grad = shard_of(f, fx, fy, fd).reshape(-1, d)
    ex, ey, vx, up_grad = fence(ex, ey, vx, up_grad)
    f = added(n0[0], ex, ey, *zr)
    fx, fy = beside_x(f), beside_y(f)
    vectors = vectors + vx
    vy = beside_y(vectors)
    fx, fy, vy = fence(fx, fy, vy)
    fd = beside_x(fy)
    vectors = vectors + vy
    vc = across(vectors)
    fd, vc = fence(fd, vc)
    vectors = vectors + vc
    vz = zs(vectors)
    vectors = (vectors + vz[0]) + (vz[1] + vz[2])
    last = shard_of(f, fx, fy, fd)
    qkv_grad = last[:, : 3 * PART].reshape(4, 3, PART, d).swapaxes(0, 1).reshape(3, -1, d)
    up_bias_grad = last[:, 96, :PAIR].reshape(-1)
    qv_bias_grad = jnp.stack([last[:, 96, at : at + PART].reshape(-1) for at in (PAIR, 2 * PAIR)])
    out_grad = last[:, PIECE:].reshape(-1, d)
    return mixed, input_grad, qkv_grad, qv_bias_grad, out_grad, up_grad, up_bias_grad, down_grad, vectors


def body(tokens, qkv_weight, qv_bias, out_weight, up_weight, up_bias, down_weight, norm_gains, shift_vectors, lengths, cotangent):
    n, d = tokens.shape
    place, row = lax.axis_index("mp"), lax.axis_index("rows")
    endings = jnp.cumsum(lax.dynamic_slice_in_dim(lengths, place, 1, 0)[0])
    position = jnp.arange(SLOTS, dtype=jnp.int32)
    segment = jnp.sum((position[:, None] >= endings[None, :]).astype(jnp.int32), axis=1)
    live = (segment < DOCS).astype(F32)[:, None]
    ident = jnp.where(segment < DOCS, segment, DOCS + position).astype(jnp.int32)
    layer = small_mesh if (lax.axis_size("rows"), lax.axis_size("mp")) == (4, 8) else any_mesh
    mixed, input_grad, qkv_grad, qv_bias_grad, out_grad, up_grad, up_bias_grad, down_grad, vectors = layer(
        tokens, jnp.swapaxes(qkv_weight, 1, 2), qv_bias, out_weight, up_weight.T, up_bias, down_weight,
        norm_gains.astype(F32), shift_vectors.astype(F32), live, ident.reshape(n, 1), ident.reshape(1, n), cotangent,
    )
    share = d // lax.axis_size("mp")
    vector_grad = lax.dynamic_slice_in_dim(vectors[:6], place * share, share, 1)
    block_loss = lax.dynamic_slice_in_dim(vectors[6], row * lax.axis_size("mp"), lax.axis_size("mp"), 0)
    return (
        mixed, block_loss, input_grad, jnp.swapaxes(qkv_grad, 1, 2), qv_bias_grad, out_grad,
        up_grad.T, up_bias_grad, down_grad, vector_grad,
    )


def solution(mesh):
    placed = (
        P(("rows", "mp"), None),
        P(None, None, "mp"),
        P(None, "mp"),
        P("mp", None),
        P(None, "mp"),
        P("mp"),
        P("mp", None),
        P(),
        P(),
        P("rows", None),
        P(("rows", "mp"), None),
    )
    return jax.shard_map(
        body,
        mesh=mesh,
        in_specs=placed,
        out_specs=(
            P(("rows", "mp"), None),
            P("rows"),
            P(("rows", "mp"), None),
            P(None, None, "mp"),
            P(None, "mp"),
            P("mp", None),
            P(None, "mp"),
            P("mp"),
            P("mp", None),
            P(None, "mp"),
        ),
        check_vma=False,
    )
```

time: 2470 us -> 517 us (0.21)
  waiting for transfers between devices: 1740 us -> 80.2 us
  matrix products: 466 us -> 0 us
  Pallas kernels: 0 us -> 282 us
  starting transfers between devices: 0.42 us -> 92 us
  local copies, waits for them, and re-layouts: 118 us -> 27.3 us
  other arithmetic: 103 us -> 22.6 us
    reduce_scatter x5 -> x0, waiting for transfers between devices: 1040 us -> none  [the longest x1 326 us: body(): lax.psum_scatter(times_back(row_slice(hidden_grad, jnp.int32(0), share *...]
    all_gather x4 -> x0, waiting for transfers between devices: 568 us -> none  [the longest x1 154 us: body(): attn_rows = lax.all_gather(normed, 'mp', axis=0, tiled=True)]
    dot_general x130 -> x0, matrix products: 466 us -> none  [the longest x6 116 us: times_back(): lax.dot_general(left, right, (((1,), (1,)), ((), ())), preferred_element_...]
    pallas_call x0 -> x26, Pallas kernels: none -> 282 us  [the longest x19 263 us: call(): pl.pallas_call(kernel, grid=grid, in_specs=[s for _, s in ins], out_specs...]
    psum x1 -> x0, waiting for transfers between devices: 131 us -> none  [body(): lax.psum((qkv_grad, qv_bias_grad, out_grad, up_grad, up_bias_grad, down_g...]
    ppermute x0 -> x78, starting transfers between devices: none -> 92 us  [moved(): return lax.ppermute(array, axis, [(i, i ^ mask) for i in range(size)])]
    ppermute x0 -> x78, waiting for transfers between devices: none -> 80.2 us  [moved(): return lax.ppermute(array, axis, [(i, i ^ mask) for i in range(size)])]
    while x5 -> x0, local copies, waits for them, and re-layouts: 45.5 us -> none  [the longest x4 34.8 us: body(): lax.map(attend_block, (queries.reshape(shaped), key_rows.reshape(shaped),...]
  transfers between devices with their start and end apart: 10 -> 78, of which waited for: 10 -> 20; matrix products, arithmetic and copies ran while one was open for 6% -> 6% of each run, Pallas kernels for 0% -> 50%
where the time goes in v1:
time: 517 us; the launch traced here: 508 us
  Pallas kernels  282 us (55%)
  starting transfers between devices  92 us (18%)
  waiting for transfers between devices  80.2 us (16%)
  local copies, waits for them, and re-layouts  27.3 us (5%)
  other arithmetic  22.6 us (4%)
    pallas_call x19, Pallas kernels, call(): pl.pallas_call(kernel, grid=grid, in_specs=[s for _, s in ins], out_specs...  263 us
    ppermute x78, starting transfers between devices, moved(): return lax.ppermute(array, axis, [(i, i ^ mask) for i in range(size)])  92 us
    ppermute x78, waiting for transfers between devices, moved(): return lax.ppermute(array, axis, [(i, i ^ mask) for i in range(size)])  80.2 us
    pallas_call x7, Pallas kernels, pack(): pl.pallas_call(functools.partial(pack_kernel, plan=plan, bands=bands), in...  19.5 us
  transfers between devices with their start and end apart: 78, of which 20 were waited for; matrix products, arithmetic and copies ran while one was open for 6% of the time, Pallas kernels for 50%

profile of v1, /device:TPU:0, one launch (start us, length us, event | category | flops | bytes accessed | tf_op | source)
XLA Modules:
  0.0 507.5 jit_solution(1193010868558674276)
XLA Ops:
  4.8 3.0 collective-permute-start
  7.8 2.6 collective-permute-start.1
  15.0 2.2 pack.7
  17.3 5.7 %prep.1 = (bf16[1024,1024]{1,0:T(8,128)(2,1)}, bf16[1024,1024]{1,0:T(8,128)(2,1)}) custom-call(bf16[1024,1024]{1,0:T(8,128)(2,1)} %refs_14_.1, bf16[1024,1024]{1,0:T(8,128)(2,1)} %cot_ref.1, f32[1024,1]{1,0:T(8,128)} %compare_convert_fusion.live_ref, f32[2,1024]{1,0:T(2,128)} %convert_element_type.203.gain_ref.refs_7_.refs_16_, ...), custom_call_target="tpu_custom_call" | custom-call | flops 1000000000 | bytes 8417280 | tf_op jit(solution)/shard_map/prep/pallas_call | solution.py:38
  23.0 6.5 %attend.4 = (bf16[1024,128]{1,0:T(8,128)(2,1)}, bf16[1024,128]{1,0:T(8,128)(2,1)}, bf16[1024,128]{1,0:T(8,128)(2,1)}, bf16[1024,128]{1,0:T(8,128)(2,1)}, f32[1,2,1024]{2,1,0:T(2,128)}) custom-call(s32[1024,1]{1,0:T(8,128)} %compare_select_fusion.col_ref, s32[1,1024]{1,0:T(1,128)} %compare_select_fusion.1.row_ref, ...), custom_call_target="tpu_custom_call" | custom-call | flops 4000000000 | bytes 4079616 | tf_op jit(solution)/shard_map/attend/pallas_call | solution.py:38
  32.3 2.0 pack.8.refs_1_
  38.4 8.5 %collective-permute-done.5.refs_0_ = bf16[160,1024]{1,0:T(8,128)(2,1)S(1)} collective-permute-done((bf16[160,1024]{1,0:T(8,128)(2,1)S(1)}, bf16[160,1024]{1,0:T(8,128)(2,1)S(1)}, u32[]{:S(2)}, u32[]{:S(2)}) %collective-permute-start.5) | collective-permute-done | bytes 327712 | tf_op jit(solution)/shard_map/ppermute | solution.py:536
  46.8 2.4 collective-permute-start.6
  49.2 13.8 %collective-permute-done.6.refs_1_ = bf16[160,1024]{1,0:T(8,128)(2,1)S(1)} collective-permute-done((bf16[160,1024]{1,0:T(8,128)(2,1)S(1)}, bf16[160,1024]{1,0:T(8,128)(2,1)S(1)}, u32[]{:S(2)}, u32[]{:S(2)}) %collective-permute-start.6) | collective-permute-done | bytes 327712 | tf_op jit(solution)/shard_map/ppermute | solution.py:536
  64.3 3.5 collective-permute-start.11
  67.8 4.4 collective-permute-done.9.refs_4_
  72.2 3.0 collective-permute-done.11.refs_2_
  76.1 3.4 pack.9
  79.6 2.1 pack.10.refs_1_
  84.8 5.8 %collective-permute-start.15 = (bf16[128,1024]{1,0:T(8,128)(2,1)S(1)}, bf16[128,1024]{1,0:T(8,128)(2,1)S(1)}, u32[]{:S(2)}, u32[]{:S(2)}) collective-permute-start(bf16[128,1024]{1,0:T(8,128)(2,1)S(1)} %dynamic-slice_bitcast_fusion), channel_id=1, source_target_pairs={{0,2},{1,3},{2,0},{3,1},{4,6},{5,7},{6,4},{7,5},{8,10},{9,11},{10,... | collective-permute-start | bytes 786440 | tf_op jit(solution)/shard_map/ppermute | solution.py:536
  90.7 14.2 %attend.5 = (bf16[1024,384]{1,0:T(8,128)(2,1)}, bf16[1024,384]{1,0:T(8,128)(2,1)}, bf16[1024,384]{1,0:T(8,128)(2,1)}, bf16[1024,384]{1,0:T(8,128)(2,1)}, f32[3,2,1024]{2,1,0:T(2,128)}) custom-call(s32[1024,1]{1,0:T(8,128)} %compare_select_fusion.col_ref, s32[1,1024]{1,0:T(1,128)} %compare_select_fusion.1.row_ref, ...), custom_call_target="tpu_custom_call" | custom-call | flops 12000000000 | bytes 8945664 | tf_op jit(solution)/shard_map/attend/pallas_call | solution.py:38
  109.6 3.5 collective-permute-start.19
  113.2 14.6 %attend.6 = (bf16[1024,384]{1,0:T(8,128)(2,1)}, bf16[1024,384]{1,0:T(8,128)(2,1)}, bf16[1024,384]{1,0:T(8,128)(2,1)}, bf16[1024,384]{1,0:T(8,128)(2,1)}, f32[3,2,1024]{2,1,0:T(2,128)}) custom-call(s32[1024,1]{1,0:T(8,128)} %compare_select_fusion.col_ref, s32[1,1024]{1,0:T(1,128)} %compare_select_fusion.1.row_ref, ...), custom_call_target="tpu_custom_call" | custom-call | flops 12000000000 | bytes 8945664 | tf_op jit(solution)/shard_map/attend/pallas_call | solution.py:38
  128.9 4.0 pack.12
  133.0 2.0 pack.11.refs_1_
  138.5 6.5 %attend.7 = (bf16[1024,128]{1,0:T(8,128)(2,1)}, bf16[1024,128]{1,0:T(8,128)(2,1)}, bf16[1024,128]{1,0:T(8,128)(2,1)}, bf16[1024,128]{1,0:T(8,128)(2,1)}, f32[1,2,1024]{2,1,0:T(2,128)}) custom-call(s32[1024,1]{1,0:T(8,128)} %compare_select_fusion.col_ref, s32[1,1024]{1,0:T(1,128)} %compare_select_fusion.1.row_ref, ...), custom_call_target="tpu_custom_call" | custom-call | flops 4000000000 | bytes 6832128 | tf_op jit(solution)/shard_map/attend/pallas_call | solution.py:38
  144.9 8.2 %join.1 = (f32[1024,1024]{1,0:T(8,128)}, bf16[1024,1024]{1,0:T(8,128)(2,1)}) custom-call(bf16[1024,1024]{1,0:T(8,128)(2,1)} %refs_14_.1, bf16[1024,128]{1,0:T(8,128)(2,1)} %get-tuple-element.257.refs_1_.o_ref.oa_ref, bf16[1024,384]{1,0:T(8,128)(2,1)} %get-tuple-element.258.refs_2_.o_ref.oa_ref, bf16[1024,128]{1,0:T(8,128)(2,1)} %get-tuple-element.260.refs_3_.o_ref, ...), custom_call_target="tpu_custom_call" | custom-call | flops 4000000000 | bytes 20996096 | tf_op jit(solution)/shard_map/join/pallas_call | solution.py:38
  153.1 2.1 collective-permute-done.20.refs_2_
  157.7 12.1 %up.2 = (bf16[1024,2048]{1,0:T(8,128)(2,1)}, bf16[1024,2048]{1,0:T(8,128)(2,1)}) custom-call(bf16[1024,1024]{1,0:T(8,128)(2,1)} %get-tuple-element.272.h_ref.ra_ref, bf16[4,4,160,1024]{3,2,1,0:T(8,128)(2,1)} %collective-permute-done.22.refs_6_.w_ref.ub_ref.wo_ref, bf16[1,2048]{1,0:T(2,128)(2,1)} %bitcast.103), custom_call_target="tpu_custom_call" | custom-call | flops 6000000000 | bytes 15732736 | tf_op jit(solution)/shard_map/up/pallas_call | solution.py:38
  170.7 3.7 pack.13.wa_ref.da_ref
  176.9 12.3 %up.3 = (bf16[1024,2048]{1,0:T(8,128)(2,1)}, bf16[1024,2048]{1,0:T(8,128)(2,1)}) custom-call(bf16[1024,1024]{1,0:T(8,128)(2,1)} %get-tuple-element.272.h_ref.ra_ref, bf16[4,4,160,1024]{3,2,1,0:T(8,128)(2,1)} %bitcast.80, bf16[1,2048]{1,0:T(2,128)(2,1)} %bitcast.104), custom_call_target="tpu_custom_call" | custom-call | flops 6000000000 | bytes 15732736 | tf_op jit(solution)/shard_map/up/pallas_call | solution.py:38
  189.2 3.1 collective-permute-done.28.ob_ref
  192.3 18.8 %outer.2 = (bf16[512,1024]{1,0:T(8,128)(2,1)}, bf16[512,1024]{1,0:T(8,128)(2,1)}, bf16[512,1024]{1,0:T(8,128)(2,1)}, bf16[256,1024]{1,0:T(8,128)(2,1)}, bf16[256,1024]{1,0:T(8,128)(2,1)}, /*index=5*/f32[1,2048]{1,0:T(1,128)}) custom-call(bf16[1024,2048]{1,0:T(8,128)(2,1)} %get-tuple-element.274.la_ref.aa_ref, ...), custom_call_target="tpu_custom_call" | custom-call | flops 8999999488 | bytes 16785408 | tf_op jit(solution)/shard_map/outer/pallas_call | solution.py:38
  216.4 18.4 %down.1 = (bf16[1024,1024]{1,0:T(8,128)(2,1)}, f32[8,128]{1,0:T(8,128)}) custom-call(bf16[1024,2048]{1,0:T(8,128)(2,1)} %get-tuple-element.274.la_ref.aa_ref, bf16[1024,2048]{1,0:T(8,128)(2,1)} %get-tuple-element.271.ab_ref, bf16[2048,1024]{1,0:T(8,128)(2,1)} %pack.13.wa_ref.da_ref, bf16[2048,1024]{1,0:T(8,128)(2,1)} %copy-done.64, ...), custom_call_target="tpu_custom_call" | custom-call | flops 8999999488 | bytes 25186304 | tf_op jit(solution)/shard_map/down/pallas_call | solution.py:38
  236.9 33.3 %back.1 = (bf16[1024,2048]{1,0:T(8,128)(2,1)}, bf16[1024,2048]{1,0:T(8,128)(2,1)}, f32[1024,1024]{1,0:T(8,128)}, bf16[1024,1024]{1,0:T(8,128)(2,1)}, f32[8,1024]{1,0:T(8,128)}) custom-call(bf16[1024,1024]{1,0:T(8,128)(2,1)} %get-tuple-element.230.ra_ref.gf_ref, bf16[1024,2048]{1,0:T(8,128)(2,1)} %get-tuple-element.295.sa_ref, ...), custom_call_target="tpu_custom_call" | custom-call | flops 19000000512 | bytes 48275456 | tf_op jit(solution)/shard_map/back/pallas_call | solution.py:38
  273.1 2.7 collective-permute-start.34
  278.4 19.4 %attend_back.4 = (bf16[1024,384]{1,0:T(8,128)(2,1)}, bf16[1024,384]{1,0:T(8,128)(2,1)}, bf16[1024,384]{1,0:T(8,128)(2,1)}) custom-call(s32[1024,1]{1,0:T(8,128)} %compare_select_fusion.col_ref, s32[1,1024]{1,0:T(1,128)} %compare_select_fusion.1.row_ref, bf16[1024,1024]{1,0:T(8,128)(2,1)} %get-tuple-element.371.ga_ref, ...), custom_call_target="tpu_custom_call" | custom-call | flops 15000000512 | bytes 12877824 | tf_op jit(solution)/shard_map/attend_back/pallas_call | solution.py:38
  301.3 16.2 %outer.3 = (bf16[512,1024]{1,0:T(8,128)(2,1)}, bf16[512,1024]{1,0:T(8,128)(2,1)}, bf16[512,1024]{1,0:T(8,128)(2,1)}, bf16[256,1024]{1,0:T(8,128)(2,1)}, bf16[256,1024]{1,0:T(8,128)(2,1)}, /*index=5*/f32[1,2048]{1,0:T(1,128)}) custom-call(bf16[1024,2048]{1,0:T(8,128)(2,1)} %get-tuple-element.319.la_ref, bf16[1024,2048]{1,0:T(8,128)(2,1)} %collective-permute-done.37.lb_ref, ...), custom_call_target="tpu_custom_call" | custom-call | flops 8999999488 | bytes 16785408 | tf_op jit(solution)/shard_map/outer/pallas_call | solution.py:38
  321.5 19.2 %attend_back.5 = (bf16[1024,384]{1,0:T(8,128)(2,1)}, bf16[1024,384]{1,0:T(8,128)(2,1)}, bf16[1024,384]{1,0:T(8,128)(2,1)}) custom-call(s32[1024,1]{1,0:T(8,128)} %compare_select_fusion.col_ref, s32[1,1024]{1,0:T(1,128)} %compare_select_fusion.1.row_ref, bf16[1024,1024]{1,0:T(8,128)(2,1)} %get-tuple-element.371.ga_ref, bf16[4,4,160,1024]{3,2,1,0:T(8,128)(2,1)} %bitcast.82, ...), custom_call_target="tpu_custom_call" | custom-call | flops 15000000512 | bytes 12877824 | tf_op jit(solution)/shard_map/attend_back/pallas_call | solution.py:38
  344.5 7.9 %attend_back.6 = (bf16[1024,128]{1,0:T(8,128)(2,1)}, bf16[1024,128]{1,0:T(8,128)(2,1)}, bf16[1024,128]{1,0:T(8,128)(2,1)}) custom-call(s32[1024,1]{1,0:T(8,128)} %compare_select_fusion.col_ref, s32[1,1024]{1,0:T(1,128)} %compare_select_fusion.1.row_ref, bf16[1024,1024]{1,0:T(8,128)(2,1)} %get-tuple-element.371.ga_ref, ...), custom_call_target="tpu_custom_call" | custom-call | flops 5000000000 | bytes 9191424 | tf_op jit(solution)/shard_map/attend_back/pallas_call | solution.py:38
  352.4 12.9 %outer_attn.2 = (bf16[432,1024]{1,0:T(8,128)(2,1)}, bf16[432,1024]{1,0:T(8,128)(2,1)}, bf16[432,1024]{1,0:T(8,128)(2,1)}, bf16[432,1024]{1,0:T(8,128)(2,1)}) custom-call(bf16[1024,384]{1,0:T(8,128)(2,1)} %get-tuple-element.343.qa_ref.refs_3_, bf16[1024,384]{1,0:T(8,128)(2,1)} %copy-done.68, bf16[1024,384]{1,0:T(8,128)(2,1)} %get-tuple-element.345.ka_ref.refs_4_, ...), custom_call_target="tpu_custom_call" | custom-call | flops 7500000256 | bytes 18268160 | tf_op jit(solution)/shard_map/outer_attn/pallas_call | solution.py:38
  368.4 4.8 collective-permute-start.49
  378.5 4.2 collective-permute-done.49
  382.7 11.9 %collective-permute-done.50 = bf16[128,1024]{1,0:T(8,128)(2,1)S(1)} collective-permute-done((bf16[128,1024]{1,0:T(8,128)(2,1)S(1)}, bf16[128,1024]{1,0:T(8,128)(2,1)S(1)}, u32[]{:S(2)}, u32[]{:S(2)}) %collective-permute-start.50) | collective-permute-done | bytes 262176 | tf_op jit(solution)/shard_map/ppermute | solution.py:536
  395.1 7.9 %attend_back.7 = (bf16[1024,128]{1,0:T(8,128)(2,1)}, bf16[1024,128]{1,0:T(8,128)(2,1)}, bf16[1024,128]{1,0:T(8,128)(2,1)}) custom-call(s32[1024,1]{1,0:T(8,128)} %compare_select_fusion.col_ref, s32[1,1024]{1,0:T(1,128)} %compare_select_fusion.1.row_ref, bf16[1024,1024]{1,0:T(8,128)(2,1)} %get-tuple-element.371.ga_ref, bf16[4,4,160,1024]{3,2,1,0:T(8,128)(2,1)} %bitcast.83, ...), custom_call_target="tpu_custom_call" | custom-call | flops 5000000000 | bytes 9191424 | tf_op jit(solution)/shard_map/attend_back/pallas_call | solution.py:38
  414.5 7.5 %outer_attn.3 = (bf16[144,1024]{1,0:T(8,128)(2,1)}, bf16[144,1024]{1,0:T(8,128)(2,1)}, bf16[144,1024]{1,0:T(8,128)(2,1)}, bf16[144,1024]{1,0:T(8,128)(2,1)}) custom-call(bf16[1024,128]{1,0:T(8,128)(2,1)} %get-tuple-element.386.qa_ref.refs_0_, bf16[1024,128]{1,0:T(8,128)(2,1)} %copy-done.46, bf16[1024,128]{1,0:T(8,128)(2,1)} %get-tuple-element.388.ka_ref.refs_1_, ...), custom_call_target="tpu_custom_call" | custom-call | flops 2500000000 | bytes 11681792 | tf_op jit(solution)/shard_map/outer_attn/pallas_call | solution.py:38
  422.0 10.3 %collective-permute-done.57 = bf16[128,1024]{1,0:T(8,128)(2,1)S(1)} collective-permute-done((bf16[128,1024]{1,0:T(8,128)(2,1)S(1)}, bf16[128,1024]{1,0:T(8,128)(2,1)S(1)}, u32[]{:S(2)}, u32[]{:S(2)}) %collective-permute-start.57) | collective-permute-done | bytes 262176 | tf_op jit(solution)/shard_map/ppermute | solution.py:536
  439.7 3.5 collective-permute-start.62
  447.4 20.9 %finish.1 = (f32[1024,1024]{1,0:T(8,128)}, f32[8,1024]{1,0:T(8,128)}) custom-call(bf16[1024,128]{1,0:T(8,128)(2,1)} %get-tuple-element.386.qa_ref.refs_0_, bf16[1024,128]{1,0:T(8,128)(2,1)} %get-tuple-element.388.ka_ref.refs_1_, bf16[1024,128]{1,0:T(8,128)(2,1)} %get-tuple-element.390.va_ref.refs_2_, bf16[1024,384]{1,0:T(8,128)(2,1)} %get-tuple-element.343.qa_ref.refs_3_, ...), custom_call_target="tpu_custom_call" | custom-call | flops 10000000000 | bytes 24158208 | tf_op jit(solution)/shard_map/finish/pallas_call | solution.py:38
  472.9 3.3 collective-permute-done.69
  481.5 4.7 collective-permute-done.72
  491.8 2.1 collective-permute-done.73
  493.9 5.3 %collective-permute-start.76 = (f32[8,1024]{1,0:T(8,128)S(1)}, f32[8,1024]{1,0:T(8,128)S(1)}, u32[]{:S(2)}, u32[]{:S(2)}) collective-permute-start(f32[8,1024]{1,0:T(8,128)S(1)} %add.170), channel_id=1, source_target_pairs={{0,4},{1,5},{2,6},{3,7},{4,0},{5,1},{6,2},{7,3},{8,12},{9,13},{10,... | collective-permute-start | bytes 98312 | tf_op jit(solution)/shard_map/ppermute | solution.py:536
  (383 shorter events, 113.5 us)
Async XLA Ops:
  4.8 27.0 %collective-permute-start = (bf16[112,1024]{1,0:T(8,128)(2,1)}, bf16[112,1024]{1,0:T(8,128)(2,1)}, u32[]{:S(2)}, u32[]{:S(2)}) collective-permute-start(bf16[112,1024]{1,0:T(8,128)(2,1)} %dynamic-slice_bitcast_fusion.1), channel_id=1, source_target_pairs={{0,2},{1,3},{2,0},{3,1},{4,6},{5,7},{6,4},{7,5},{8,10},{9,11},{10,... | collective-permute-start | bytes 688136 | tf_op jit(solution)/shard_map/ppermute | solution.py:536
  7.8 24.0 %collective-permute-start.1 = (bf16[112,1024]{1,0:T(8,128)(2,1)}, bf16[112,1024]{1,0:T(8,128)(2,1)}, u32[]{:S(2)}, u32[]{:S(2)}) collective-permute-start(bf16[112,1024]{1,0:T(8,128)(2,1)} %dynamic-slice_bitcast_fusion.1), channel_id=1, source_target_pairs={{0,4},{1,5},{2,6},{3,7},{4,0},{5,1},{6,2},{7,3},{8,12},{9,13},{10,... | collective-permute-start | bytes 688136 | tf_op jit(solution)/shard_map/ppermute | solution.py:536
  10.4 21.4 %collective-permute-start.2 = (bf16[112,1024]{1,0:T(8,128)(2,1)}, bf16[112,1024]{1,0:T(8,128)(2,1)}, u32[]{:S(2)}, u32[]{:S(2)}) collective-permute-start(bf16[112,1024]{1,0:T(8,128)(2,1)} %dynamic-slice_bitcast_fusion.1), channel_id=1, source_target_pairs={{0,6},{1,7},{2,4},{3,5},{4,2},{5,3},{6,0},{7,1},{8,14},{9,15},{10,... | collective-permute-start | bytes 688136 | tf_op jit(solution)/shard_map/ppermute | solution.py:536
  31.8 31.3 %collective-permute-start.7 = (bf16[1024,1024]{1,0:T(8,128)(2,1)S(1)}, bf16[1024,1024]{1,0:T(8,128)(2,1)S(1)}, u32[]{:S(2)}, u32[]{:S(2)}) collective-permute-start(bf16[1024,1024]{1,0:T(8,128)(2,1)S(1)} %copy-done.5), channel_id=1, source_target_pairs={{0,1},{1,0},{2,3},{3,2},{4,5},{5,4},{6,7},{7,6},{8,9},{9,8},{10,11... | collective-permute-start | bytes 6291464 | tf_op jit(solution)/shard_map/ppermute | solution.py:536
  31.9 31.3 %collective-permute-start.8 = (bf16[1024,1024]{1,0:T(8,128)(2,1)}, bf16[1024,1024]{1,0:T(8,128)(2,1)}, u32[]{:S(2)}, u32[]{:S(2)}) collective-permute-start(bf16[1024,1024]{1,0:T(8,128)(2,1)} %get-tuple-element.230.ra_ref.gf_ref), channel_id=1, source_target_pairs={{0,1},{1,0},{2,3},{3,2},{4,5},{5,4},{6,7},{7,6},{8,9},{9,8},{10,11... | collective-permute-start | bytes 6291464 | tf_op jit(solution)/shard_map/ppermute | solution.py:536
  34.4 28.7 %collective-permute-start.3 = (bf16[336,1024]{1,0:T(8,128)(2,1)}, bf16[336,1024]{1,0:T(8,128)(2,1)S(1)}, u32[]{:S(2)}, u32[]{:S(2)}) collective-permute-start(bf16[336,1024]{1,0:T(8,128)(2,1)} %pack.8.refs_1_), channel_id=1, source_target_pairs={{0,8},{8,0},{16,24},{24,16},{1,9},{9,1},{17,25},{25,17},{2,10},{10... | collective-permute-start | bytes 2064392 | tf_op jit(solution)/shard_map/ppermute | solution.py:536
  36.2 26.9 %collective-permute-start.4 = (bf16[336,1024]{1,0:T(8,128)(2,1)}, bf16[336,1024]{1,0:T(8,128)(2,1)S(1)}, u32[]{:S(2)}, u32[]{:S(2)}) collective-permute-start(bf16[336,1024]{1,0:T(8,128)(2,1)} %pack.8.refs_1_), channel_id=1, source_target_pairs={{0,16},{8,24},{16,0},{24,8},{1,17},{9,25},{17,1},{25,9},{2,18},{10... | collective-permute-start | bytes 2064392 | tf_op jit(solution)/shard_map/ppermute | solution.py:536
  79.5 27.9 %collective-permute-start.12 = (bf16[4,4,112,1024]{3,2,1,0:T(8,128)(2,1)}, bf16[4,4,112,1024]{3,2,1,0:T(8,128)(2,1)}, u32[]{:S(2)}, u32[]{:S(2)}) collective-permute-start(bf16[4,4,112,1024]{3,2,1,0:T(8,128)(2,1)} %bitcast.84), channel_id=1, source_target_pairs={{0,1},{1,0},{2,3},{3,2},{4,5},{5,4},{6,7},{7,6},{8,9},{9,8},{10,11... | collective-permute-start | bytes 11010056 | tf_op jit(solution)/shard_map/ppermute | solution.py:536
  81.7 24.4 %collective-permute-start.13 = (bf16[480,1024]{1,0:T(8,128)(2,1)}, bf16[480,1024]{1,0:T(8,128)(2,1)S(1)}, u32[]{:S(2)}, u32[]{:S(2)}) collective-permute-start(bf16[480,1024]{1,0:T(8,128)(2,1)} %pack.10.refs_1_), channel_id=1, source_target_pairs={{0,8},{8,0},{16,24},{24,16},{1,9},{9,1},{17,25},{25,17},{2,10},{10... | collective-permute-start | bytes 2949128 | tf_op jit(solution)/shard_map/ppermute | solution.py:536
  83.3 24.1 %collective-permute-start.14 = (bf16[480,1024]{1,0:T(8,128)(2,1)}, bf16[480,1024]{1,0:T(8,128)(2,1)S(1)}, u32[]{:S(2)}, u32[]{:S(2)}) collective-permute-start(bf16[480,1024]{1,0:T(8,128)(2,1)} %pack.10.refs_1_), channel_id=1, source_target_pairs={{0,16},{8,24},{16,0},{24,8},{1,17},{9,25},{17,1},{25,9},{2,18},{10... | collective-permute-start | bytes 2949128 | tf_op jit(solution)/shard_map/ppermute | solution.py:536
  84.8 20.0 %collective-permute-start.15 = (bf16[128,1024]{1,0:T(8,128)(2,1)S(1)}, bf16[128,1024]{1,0:T(8,128)(2,1)S(1)}, u32[]{:S(2)}, u32[]{:S(2)}) collective-permute-start(bf16[128,1024]{1,0:T(8,128)(2,1)S(1)} %dynamic-slice_bitcast_fusion), channel_id=1, source_target_pairs={{0,2},{1,3},{2,0},{3,1},{4,6},{5,7},{6,4},{7,5},{8,10},{9,11},{10,... | collective-permute-start | bytes 786440 | tf_op jit(solution)/shard_map/ppermute | solution.py:536
  107.4 20.5 %collective-permute-start.17 = (bf16[240,1024]{1,0:T(8,128)(2,1)S(1)}, bf16[240,1024]{1,0:T(8,128)(2,1)S(1)}, u32[]{:S(2)}, u32[]{:S(2)}) collective-permute-start(bf16[240,1024]{1,0:T(8,128)(2,1)S(1)} %slice.186), channel_id=1, source_target_pairs={{0,8},{8,0},{16,24},{24,16},{1,9},{9,1},{17,25},{25,17},{2,10},{10... | collective-permute-start | bytes 1474568 | tf_op jit(solution)/shard_map/ppermute | solution.py:536
  108.0 19.8 %collective-permute-start.18 = (bf16[240,1024]{1,0:T(8,128)(2,1)S(1)}, bf16[240,1024]{1,0:T(8,128)(2,1)S(1)}, u32[]{:S(2)}, u32[]{:S(2)}) collective-permute-start(bf16[240,1024]{1,0:T(8,128)(2,1)S(1)} %slice.187), channel_id=1, source_target_pairs={{0,16},{8,24},{16,0},{24,8},{1,17},{9,25},{17,1},{25,9},{2,18},{10... | collective-permute-start | bytes 1474568 | tf_op jit(solution)/shard_map/ppermute | solution.py:536
  109.6 18.2 %collective-permute-start.19 = (bf16[128,1024]{1,0:T(8,128)(2,1)S(1)}, bf16[128,1024]{1,0:T(8,128)(2,1)S(1)}, u32[]{:S(2)}, u32[]{:S(2)}) collective-permute-start(bf16[128,1024]{1,0:T(8,128)(2,1)S(1)} %dynamic-slice_bitcast_fusion), channel_id=1, source_target_pairs={{0,6},{1,7},{2,4},{3,5},{4,2},{5,3},{6,0},{7,1},{8,14},{9,15},{10,... | collective-permute-start | bytes 786440 | tf_op jit(solution)/shard_map/ppermute | solution.py:536
  135.0 20.2 %collective-permute-start.20 = (bf16[384,1024]{1,0:T(8,128)(2,1)}, bf16[384,1024]{1,0:T(8,128)(2,1)S(1)}, u32[]{:S(2)}, u32[]{:S(2)}) collective-permute-start(bf16[384,1024]{1,0:T(8,128)(2,1)} %pack.11.refs_1_), channel_id=1, source_target_pairs={{0,8},{8,0},{16,24},{24,16},{1,9},{9,1},{17,25},{25,17},{2,10},{10... | collective-permute-start | bytes 2359304 | tf_op jit(solution)/shard_map/ppermute | solution.py:536
  136.6 19.9 %collective-permute-start.21 = (bf16[384,1024]{1,0:T(8,128)(2,1)}, bf16[384,1024]{1,0:T(8,128)(2,1)S(1)}, u32[]{:S(2)}, u32[]{:S(2)}) collective-permute-start(bf16[384,1024]{1,0:T(8,128)(2,1)} %pack.11.refs_1_), channel_id=1, source_target_pairs={{0,16},{8,24},{16,0},{24,8},{1,17},{9,25},{17,1},{25,9},{2,18},{10... | collective-permute-start | bytes 2359304 | tf_op jit(solution)/shard_map/ppermute | solution.py:536
  211.2 23.7 %collective-permute-start.30 = (bf16[256,1024]{1,0:T(8,128)(2,1)}, bf16[256,1024]{1,0:T(8,128)(2,1)S(1)}, u32[]{:S(2)}, u32[]{:S(2)}) collective-permute-start(bf16[256,1024]{1,0:T(8,128)(2,1)} %get-tuple-element.283), channel_id=1, source_target_pairs={{0,8},{8,0},{16,24},{24,16},{1,9},{9,1},{17,25},{25,17},{2,10},{10... | collective-permute-start | bytes 1572872 | tf_op jit(solution)/shard_map/ppermute | solution.py:536
  212.7 22.1 %collective-permute-start.31 = (bf16[256,1024]{1,0:T(8,128)(2,1)}, bf16[256,1024]{1,0:T(8,128)(2,1)S(1)}, u32[]{:S(2)}, u32[]{:S(2)}) collective-permute-start(bf16[256,1024]{1,0:T(8,128)(2,1)} %get-tuple-element.284), channel_id=1, source_target_pairs={{0,16},{8,24},{16,0},{24,8},{1,17},{9,25},{17,1},{25,9},{2,18},{10... | collective-permute-start | bytes 1572872 | tf_op jit(solution)/shard_map/ppermute | solution.py:536
  235.1 35.0 %collective-permute-start.32 = (bf16[512,1024]{1,0:T(8,128)(2,1)S(1)}, bf16[512,1024]{1,0:T(8,128)(2,1)S(1)}, u32[]{:S(2)}, u32[]{:S(2)}) collective-permute-start(bf16[512,1024]{1,0:T(8,128)(2,1)S(1)} %pad_maximum_fusion.1), channel_id=1, source_target_pairs={{0,8},{8,0},{16,24},{24,16},{1,9},{9,1},{17,25},{25,17},{2,10},{10... | collective-permute-start | bytes 3145736 | tf_op jit(solution)/shard_map/ppermute | solution.py:536
  236.3 33.9 %collective-permute-start.33 = (bf16[512,1024]{1,0:T(8,128)(2,1)S(1)}, bf16[512,1024]{1,0:T(8,128)(2,1)S(1)}, u32[]{:S(2)}, u32[]{:S(2)}) collective-permute-start(bf16[512,1024]{1,0:T(8,128)(2,1)S(1)} %pad_maximum_fusion.2), channel_id=1, source_target_pairs={{0,16},{8,24},{16,0},{24,8},{1,17},{9,25},{17,1},{25,9},{2,18},{10... | collective-permute-start | bytes 3145736 | tf_op jit(solution)/shard_map/ppermute | solution.py:536
  270.2 27.6 %collective-permute-start.37 = (bf16[1024,2048]{1,0:T(8,128)(2,1)}, bf16[1024,2048]{1,0:T(8,128)(2,1)}, u32[]{:S(2)}, u32[]{:S(2)}) collective-permute-start(bf16[1024,2048]{1,0:T(8,128)(2,1)} %get-tuple-element.304), channel_id=1, source_target_pairs={{0,1},{1,0},{2,3},{3,2},{4,5},{5,4},{6,7},{7,6},{8,9},{9,8},{10,11... | collective-permute-start | bytes 12582920 | tf_op jit(solution)/shard_map/ppermute | solution.py:536
  271.2 26.6 %collective-permute-start.38 = (bf16[1024,1024]{1,0:T(8,128)(2,1)}, bf16[1024,1024]{1,0:T(8,128)(2,1)S(1)}, u32[]{:S(2)}, u32[]{:S(2)}) collective-permute-start(bf16[1024,1024]{1,0:T(8,128)(2,1)} %get-tuple-element.371.ga_ref), channel_id=1, source_target_pairs={{0,1},{1,0},{2,3},{3,2},{4,5},{5,4},{6,7},{7,6},{8,9},{9,8},{10,11... | collective-permute-start | bytes 6291464 | tf_op jit(solution)/shard_map/ppermute | solution.py:536
  273.1 24.7 %collective-permute-start.34 = (bf16[128,1024]{1,0:T(8,128)(2,1)S(1)}, bf16[128,1024]{1,0:T(8,128)(2,1)S(1)}, u32[]{:S(2)}, u32[]{:S(2)}) collective-permute-start(bf16[128,1024]{1,0:T(8,128)(2,1)S(1)} %get-tuple-element.473), channel_id=1, source_target_pairs={{0,2},{1,3},{2,0},{3,1},{4,6},{5,7},{6,4},{7,5},{8,10},{9,11},{10,... | collective-permute-start | bytes 786440 | tf_op jit(solution)/shard_map/ppermute | solution.py:536
  275.7 22.0 %collective-permute-start.35 = (bf16[128,1024]{1,0:T(8,128)(2,1)S(1)}, bf16[128,1024]{1,0:T(8,128)(2,1)S(1)}, u32[]{:S(2)}, u32[]{:S(2)}) collective-permute-start(bf16[128,1024]{1,0:T(8,128)(2,1)S(1)} %get-tuple-element.472), channel_id=1, source_target_pairs={{0,4},{1,5},{2,6},{3,7},{4,0},{5,1},{6,2},{7,3},{8,12},{9,13},{10,... | collective-permute-start | bytes 786440 | tf_op jit(solution)/shard_map/ppermute | solution.py:536
  277.0 20.8 %collective-permute-start.36 = (bf16[128,1024]{1,0:T(8,128)(2,1)S(1)}, bf16[128,1024]{1,0:T(8,128)(2,1)S(1)}, u32[]{:S(2)}, u32[]{:S(2)}) collective-permute-start(bf16[128,1024]{1,0:T(8,128)(2,1)S(1)} %get-tuple-element.471), channel_id=1, source_target_pairs={{0,6},{1,7},{2,4},{3,5},{4,2},{5,3},{6,0},{7,1},{8,14},{9,15},{10,... | collective-permute-start | bytes 786440 | tf_op jit(solution)/shard_map/ppermute | solution.py:536
  298.0 20.8 %collective-permute-start.39 = (bf16[128,1024]{1,0:T(8,128)(2,1)S(1)}, bf16[128,1024]{1,0:T(8,128)(2,1)S(1)}, u32[]{:S(2)}, u32[]{:S(2)}) collective-permute-start(bf16[128,1024]{1,0:T(8,128)(2,1)S(1)} %add_convert_fusion.11), channel_id=1, source_target_pairs={{0,8},{8,0},{16,24},{24,16},{1,9},{9,1},{17,25},{25,17},{2,10},{10... | collective-permute-start | bytes 786440 | tf_op jit(solution)/shard_map/ppermute | solution.py:536
  299.2 19.6 %collective-permute-start.40 = (bf16[128,1024]{1,0:T(8,128)(2,1)S(1)}, bf16[128,1024]{1,0:T(8,128)(2,1)S(1)}, u32[]{:S(2)}, u32[]{:S(2)}) collective-permute-start(bf16[128,1024]{1,0:T(8,128)(2,1)S(1)} %add_convert_fusion.11), channel_id=1, source_target_pairs={{0,16},{8,24},{16,0},{24,8},{1,17},{9,25},{17,1},{25,9},{2,18},{10... | collective-permute-start | bytes 786440 | tf_op jit(solution)/shard_map/ppermute | solution.py:536
  300.7 18.1 %collective-permute-start.41 = (bf16[1024,384]{1,0:T(8,128)(2,1)}, bf16[1024,384]{1,0:T(8,128)(2,1)S(1)}, u32[]{:S(2)}, u32[]{:S(2)}) collective-permute-start(bf16[1024,384]{1,0:T(8,128)(2,1)} %get-tuple-element.316.refs_9_), channel_id=1, source_target_pairs={{0,1},{1,0},{2,3},{3,2},{4,5},{5,4},{6,7},{7,6},{8,9},{9,8},{10,11... | collective-permute-start | bytes 2359304 | tf_op jit(solution)/shard_map/ppermute | solution.py:536
  300.7 18.1 %collective-permute-start.42 = (bf16[1024,384]{1,0:T(8,128)(2,1)}, bf16[1024,384]{1,0:T(8,128)(2,1)S(1)}, u32[]{:S(2)}, u32[]{:S(2)}) collective-permute-start(bf16[1024,384]{1,0:T(8,128)(2,1)} %get-tuple-element.317.refs_10_), channel_id=1, source_target_pairs={{0,1},{1,0},{2,3},{3,2},{4,5},{5,4},{6,7},{7,6},{8,9},{9,8},{10,11... | collective-permute-start | bytes 2359304 | tf_op jit(solution)/shard_map/ppermute | solution.py:536
  318.9 22.0 %collective-permute-start.44 = (bf16[256,1024]{1,0:T(8,128)(2,1)}, bf16[256,1024]{1,0:T(8,128)(2,1)S(1)}, u32[]{:S(2)}, u32[]{:S(2)}) collective-permute-start(bf16[256,1024]{1,0:T(8,128)(2,1)} %get-tuple-element.329), channel_id=1, source_target_pairs={{0,8},{8,0},{16,24},{24,16},{1,9},{9,1},{17,25},{25,17},{2,10},{10... | collective-permute-start | bytes 1572872 | tf_op jit(solution)/shard_map/ppermute | solution.py:536
  319.8 21.1 %collective-permute-start.45 = (bf16[256,1024]{1,0:T(8,128)(2,1)}, bf16[256,1024]{1,0:T(8,128)(2,1)S(1)}, u32[]{:S(2)}, u32[]{:S(2)}) collective-permute-start(bf16[256,1024]{1,0:T(8,128)(2,1)} %get-tuple-element.330), channel_id=1, source_target_pairs={{0,16},{8,24},{16,0},{24,8},{1,17},{9,25},{17,1},{25,9},{2,18},{10... | collective-permute-start | bytes 1572872 | tf_op jit(solution)/shard_map/ppermute | solution.py:536
  320.4 20.5 %collective-permute-start.46 = (bf16[128,1024]{1,0:T(8,128)(2,1)S(1)}, bf16[128,1024]{1,0:T(8,128)(2,1)S(1)}, u32[]{:S(2)}, u32[]{:S(2)}) collective-permute-start(bf16[128,1024]{1,0:T(8,128)(2,1)S(1)} %collective-permute-done.40), channel_id=1, source_target_pairs={{0,8},{8,0},{16,24},{24,16},{1,9},{9,1},{17,25},{25,17},{2,10},{10... | collective-permute-start | bytes 786440 | tf_op jit(solution)/shard_map/ppermute | solution.py:536
  341.7 24.8 %collective-permute-start.47 = (bf16[512,1024]{1,0:T(8,128)(2,1)S(1)}, bf16[512,1024]{1,0:T(8,128)(2,1)S(1)}, u32[]{:S(2)}, u32[]{:S(2)}) collective-permute-start(bf16[512,1024]{1,0:T(8,128)(2,1)S(1)} %pad_maximum_fusion.3), channel_id=1, source_target_pairs={{0,8},{8,0},{16,24},{24,16},{1,9},{9,1},{17,25},{25,17},{2,10},{10... | collective-permute-start | bytes 3145736 | tf_op jit(solution)/shard_map/ppermute | solution.py:536
  342.9 24.8 %collective-permute-start.48 = (bf16[512,1024]{1,0:T(8,128)(2,1)S(1)}, bf16[512,1024]{1,0:T(8,128)(2,1)S(1)}, u32[]{:S(2)}, u32[]{:S(2)}) collective-permute-start(bf16[512,1024]{1,0:T(8,128)(2,1)S(1)} %pad_maximum_fusion.4), channel_id=1, source_target_pairs={{0,16},{8,24},{16,0},{24,8},{1,17},{9,25},{17,1},{25,9},{2,18},{10... | collective-permute-start | bytes 3145736 | tf_op jit(solution)/shard_map/ppermute | solution.py:536
  373.2 21.4 %collective-permute-start.50 = (bf16[128,1024]{1,0:T(8,128)(2,1)S(1)}, bf16[128,1024]{1,0:T(8,128)(2,1)S(1)}, u32[]{:S(2)}, u32[]{:S(2)}) collective-permute-start(bf16[128,1024]{1,0:T(8,128)(2,1)S(1)} %get-tuple-element.469), channel_id=1, source_target_pairs={{0,4},{1,5},{2,6},{3,7},{4,0},{5,1},{6,2},{7,3},{8,12},{9,13},{10,... | collective-permute-start | bytes 786440 | tf_op jit(solution)/shard_map/ppermute | solution.py:536
  374.5 20.1 %collective-permute-start.51 = (bf16[128,1024]{1,0:T(8,128)(2,1)S(1)}, bf16[128,1024]{1,0:T(8,128)(2,1)}, u32[]{:S(2)}, u32[]{:S(2)}) collective-permute-start(bf16[128,1024]{1,0:T(8,128)(2,1)S(1)} %get-tuple-element.468), channel_id=1, source_target_pairs={{0,6},{1,7},{2,4},{3,5},{4,2},{5,3},{6,0},{7,1},{8,14},{9,15},{10,... | collective-permute-start | bytes 786440 | tf_op jit(solution)/shard_map/ppermute | solution.py:536
  375.9 27.2 %collective-permute-start.52 = (bf16[208,1024]{1,0:T(8,128)(2,1)S(1)}, bf16[208,1024]{1,0:T(8,128)(2,1)S(1)}, u32[]{:S(2)}, u32[]{:S(2)}) collective-permute-start(bf16[208,1024]{1,0:T(8,128)(2,1)S(1)} %slice.209), channel_id=1, source_target_pairs={{0,8},{8,0},{16,24},{24,16},{1,9},{9,1},{17,25},{25,17},{2,10},{10... | collective-permute-start | bytes 1277960 | tf_op jit(solution)/shard_map/ppermute | solution.py:536
  376.9 26.3 %collective-permute-start.53 = (bf16[224,1024]{1,0:T(8,128)(2,1)S(1)}, bf16[224,1024]{1,0:T(8,128)(2,1)S(1)}, u32[]{:S(2)}, u32[]{:S(2)}) collective-permute-start(bf16[224,1024]{1,0:T(8,128)(2,1)S(1)} %slice.210), channel_id=1, source_target_pairs={{0,16},{8,24},{16,0},{24,8},{1,17},{9,25},{17,1},{25,9},{2,18},{10... | collective-permute-start | bytes 1376264 | tf_op jit(solution)/shard_map/ppermute | solution.py:536
  382.7 20.4 %collective-permute-start.54 = (bf16[1024,128]{1,0:T(8,128)(2,1)S(1)}, bf16[1024,128]{1,0:T(8,128)(2,1)S(1)}, u32[]{:S(2)}, u32[]{:S(2)}) collective-permute-start(bf16[1024,128]{1,0:T(8,128)(2,1)S(1)} %copy-done.71), channel_id=1, source_target_pairs={{0,1},{1,0},{2,3},{3,2},{4,5},{5,4},{6,7},{7,6},{8,9},{9,8},{10,11... | collective-permute-start | bytes 786440 | tf_op jit(solution)/shard_map/ppermute | solution.py:536
  404.9 29.2 %collective-permute-start.59 = (bf16[432,1024]{1,0:T(8,128)(2,1)}, bf16[432,1024]{1,0:T(8,128)(2,1)S(1)}, u32[]{:S(2)}, u32[]{:S(2)}) collective-permute-start(bf16[432,1024]{1,0:T(8,128)(2,1)} %pad_maximum_fusion.7), channel_id=1, source_target_pairs={{0,8},{8,0},{16,24},{24,16},{1,9},{9,1},{17,25},{25,17},{2,10},{10... | collective-permute-start | bytes 2654216 | tf_op jit(solution)/shard_map/ppermute | solution.py:536
  406.9 27.2 %collective-permute-start.60 = (bf16[432,1024]{1,0:T(8,128)(2,1)}, bf16[432,1024]{1,0:T(8,128)(2,1)}, u32[]{:S(2)}, u32[]{:S(2)}) collective-permute-start(bf16[432,1024]{1,0:T(8,128)(2,1)} %pad_maximum_fusion.8), channel_id=1, source_target_pairs={{0,16},{8,24},{16,0},{24,8},{1,17},{9,25},{17,1},{25,9},{2,18},{10... | collective-permute-start | bytes 2654216 | tf_op jit(solution)/shard_map/ppermute | solution.py:536
  409.6 22.7 %collective-permute-start.57 = (bf16[128,1024]{1,0:T(8,128)(2,1)S(1)}, bf16[128,1024]{1,0:T(8,128)(2,1)S(1)}, u32[]{:S(2)}, u32[]{:S(2)}) collective-permute-start(bf16[128,1024]{1,0:T(8,128)(2,1)S(1)} %add_convert_fusion.10), channel_id=1, source_target_pairs={{0,8},{8,0},{16,24},{24,16},{1,9},{9,1},{17,25},{25,17},{2,10},{10... | collective-permute-start | bytes 786440 | tf_op jit(solution)/shard_map/ppermute | solution.py:536
  410.8 23.2 %collective-permute-start.58 = (bf16[128,1024]{1,0:T(8,128)(2,1)S(1)}, bf16[128,1024]{1,0:T(8,128)(2,1)S(1)}, u32[]{:S(2)}, u32[]{:S(2)}) collective-permute-start(bf16[128,1024]{1,0:T(8,128)(2,1)S(1)} %add_convert_fusion.10), channel_id=1, source_target_pairs={{0,16},{8,24},{16,0},{24,8},{1,17},{9,25},{17,1},{25,9},{2,18},{10... | collective-permute-start | bytes 786440 | tf_op jit(solution)/shard_map/ppermute | solution.py:536
  435.9 32.5 %collective-permute-start.61 = (bf16[128,1024]{1,0:T(8,128)(2,1)S(1)}, bf16[128,1024]{1,0:T(8,128)(2,1)S(1)}, u32[]{:S(2)}, u32[]{:S(2)}) collective-permute-start(bf16[128,1024]{1,0:T(8,128)(2,1)S(1)} %collective-permute-done.58), channel_id=1, source_target_pairs={{0,8},{8,0},{16,24},{24,16},{1,9},{9,1},{17,25},{25,17},{2,10},{10... | collective-permute-start | bytes 786440 | tf_op jit(solution)/shard_map/ppermute | solution.py:536
  439.7 28.7 %collective-permute-start.62 = (bf16[144,1024]{1,0:T(8,128)(2,1)S(1)}, bf16[144,1024]{1,0:T(8,128)(2,1)S(1)}, u32[]{:S(2)}, u32[]{:S(2)}) collective-permute-start(bf16[144,1024]{1,0:T(8,128)(2,1)S(1)} %get-tuple-element.476), channel_id=1, source_target_pairs={{0,2},{1,3},{2,0},{3,1},{4,6},{5,7},{6,4},{7,5},{8,10},{9,11},{10,... | collective-permute-start | bytes 884744 | tf_op jit(solution)/shard_map/ppermute | solution.py:536
  443.2 25.3 %collective-permute-start.63 = (bf16[144,1024]{1,0:T(8,128)(2,1)S(1)}, bf16[144,1024]{1,0:T(8,128)(2,1)S(1)}, u32[]{:S(2)}, u32[]{:S(2)}) collective-permute-start(bf16[144,1024]{1,0:T(8,128)(2,1)S(1)} %get-tuple-element.475), channel_id=1, source_target_pairs={{0,4},{1,5},{2,6},{3,7},{4,0},{5,1},{6,2},{7,3},{8,12},{9,13},{10,... | collective-permute-start | bytes 884744 | tf_op jit(solution)/shard_map/ppermute | solution.py:536
  444.5 24.0 %collective-permute-start.64 = (bf16[144,1024]{1,0:T(8,128)(2,1)S(1)}, bf16[144,1024]{1,0:T(8,128)(2,1)S(1)}, u32[]{:S(2)}, u32[]{:S(2)}) collective-permute-start(bf16[144,1024]{1,0:T(8,128)(2,1)S(1)} %get-tuple-element.474), channel_id=1, source_target_pairs={{0,6},{1,7},{2,4},{3,5},{4,2},{5,3},{6,0},{7,1},{8,14},{9,15},{10,... | collective-permute-start | bytes 884744 | tf_op jit(solution)/shard_map/ppermute | solution.py:536
  445.9 22.5 %collective-permute-start.66 = (bf16[80,1024]{1,0:T(8,128)(2,1)S(1)}, bf16[80,1024]{1,0:T(8,128)(2,1)S(1)}, u32[]{:S(2)}, u32[]{:S(2)}) collective-permute-start(bf16[80,1024]{1,0:T(8,128)(2,1)S(1)} %slice.220), channel_id=1, source_target_pairs={{0,16},{8,24},{16,0},{24,8},{1,17},{9,25},{17,1},{25,9},{2,18},{10... | collective-permute-start | bytes 491528 | tf_op jit(solution)/shard_map/ppermute | solution.py:536
  (102 other events, 1087.0 us)
